TPU v7x, 32 devices: a whole 2x2x4 slice. The times are simulated.
32 devices in a mesh: gx: 8 (over z, y), gy: 4 (over x, core).
Axes of the slice: x: 2, y: 2, z: 4, core: 2. Of those that a mesh axis runs over, the one named last changes fastest.
Arguments:
- populations: float32 [27, 64, 128, 128], P(None, 'gx', 'gy'), may hold values from 0.49 to 1.69
- precursor: float32 [27, 16, 128, 128], P(None, 'gx', 'gy'), may hold values from 0.49 to 1.69
- pairing: int32 [8], replicated, may hold values from 0 to 7, each once
- rates: float32 [27], replicated, may hold values from 0.5 to 1.9
- loading: float32 [32], replicated, may hold values from 4 to 32
- disc_cols: int32 [512], replicated, may hold values from 0 to 8191, as said below
- disc_turb: int32 [512], replicated, may hold values from -1 to 31, as said below
Outputs:
- read: float32 [27, 64, 128, 128], P(None, 'gx', 'gy')
- disc_speed: float32 [32], replicated
Inputs may be any that keep to these rules, and one draw needn't show every extreme that they name: `disc_cols`: each turbine's used slots name 8 to 16 spanwise-adjacent columns (periodic in y) of one streamwise plane; unused slots hold column 0. `disc_turb`: every turbine id 0..31 has 8 to 16 used slots, both counts reached; -1 marks an unused slot; slots are in no particular order.
All inputs are finite; a program needn't handle non-finite values.
Results may differ from a plain program's by a relative error of at most 0.00009.
Values sent between devices are 32-bit elements; how exact they have to be, the bound alone decides.
A program may use at most 128 MiB of HBM per device.

v0:
```python
import jax
import jax.numpy as jnp
import numpy as np
from jax import lax
from jax.sharding import PartitionSpec as P

FULL_PRECISION = lax.Precision.HIGHEST


def extended(cells, sides, width):
    for axis, dim in sides:
        count = lax.axis_size(axis)
        head = lax.slice_in_dim(cells, 0, width, axis=dim)
        tail = lax.slice_in_dim(cells, cells.shape[dim] - width, cells.shape[dim], axis=dim)
        cells = jnp.concatenate(
            [
                lax.ppermute(tail, axis, [(i, (i + 1) % count) for i in range(count)]),
                cells,
                lax.ppermute(head, axis, [((i + 1) % count, i) for i in range(count)]),
            ],
            axis=dim,
        )
    return cells


def lattice_tables():
    steps_one = np.array([-1.0, 0.0, 1.0])
    weight_one = np.array([1.0 / 6.0, 2.0 / 3.0, 1.0 / 6.0])
    grid_x, grid_y, grid_z = np.meshgrid(np.arange(3), np.arange(3), np.arange(3), indexing="ij")
    grid_x = grid_x.ravel()
    grid_y = grid_y.ravel()
    grid_z = grid_z.ravel()
    shift_x = steps_one[grid_x]
    shift_y = steps_one[grid_y]
    shift_z = steps_one[grid_z]
    weights = weight_one[grid_x] * weight_one[grid_y] * weight_one[grid_z]
    vander = np.array([[1.0, 1.0, 1.0], [-1.0, 0.0, 1.0], [1.0, 0.0, 1.0]])
    inverse = np.array([[0.0, -0.5, 0.5], [1.0, 0.0, -1.0], [0.0, 0.5, 0.5]])
    moment_map = np.kron(np.kron(vander, vander), vander) * weights[None, :]
    back_map = np.kron(np.kron(inverse, inverse), inverse) / weights[:, None]
    third = 1.0 / 3.0
    fringe_map = np.stack(
        [
            weights,
            weights * shift_x,
            weights * shift_y,
            weights * shift_z,
            weights * shift_x * shift_x,
            weights * shift_y * shift_y,
            weights * shift_z * shift_z,
            weights * shift_x * shift_y,
            weights * shift_x * shift_z,
            weights * shift_y * shift_z,
        ]
    )
    quad_x = shift_x * shift_x - third
    quad_y = shift_y * shift_y - third
    quad_z = shift_z * shift_z - third
    rebuild_map = np.stack(
        [
            1.0 - 1.5 * (quad_x + quad_y + quad_z),
            3.0 * shift_x,
            3.0 * shift_y,
            3.0 * shift_z,
            4.5 * quad_x,
            4.5 * quad_y,
            4.5 * quad_z,
            9.0 * shift_x * shift_y,
            9.0 * shift_x * shift_z,
            9.0 * shift_y * shift_z,
        ],
        axis=1,
    )
    tables = (shift_x, shift_y, shift_z, moment_map, back_map, fringe_map, rebuild_map)
    return tuple((jnp.asarray(table, dtype=jnp.float32) for table in tables))


def disc_profile(depth):
    heights = jnp.arange(depth).astype(jnp.float32)
    return jnp.exp(-jnp.square((heights - depth / 3.0) / (depth / 6.0)))


def relax_cells(tables, moments, rates, force):
    shift_x, shift_y, shift_z, moment_map, back_map = tables[:5]
    density = moments[0]
    velocity_x = moments[9] / density
    velocity_y = moments[3] / density
    velocity_z = moments[1] / density
    projected = (
        shift_x[:, None] * velocity_x[None, :]
        + shift_y[:, None] * velocity_y[None, :]
        + shift_z[:, None] * velocity_z[None, :]
    )
    speed_sq = velocity_x * velocity_x + velocity_y * velocity_y + velocity_z * velocity_z
    balance = density[None, :] * (
        1.0 + 3.0 * projected + 4.5 * projected * projected - 1.5 * speed_sq[None, :]
    )
    balance_moments = jnp.dot(moment_map, balance, precision=FULL_PRECISION)
    relaxed = moments - rates[:, None] * (moments - balance_moments)
    return (
        jnp.dot(back_map, relaxed, precision=FULL_PRECISION)
        + 3.0 * shift_x[:, None] * force[None, :]
    )


def body(populations, precursor, pairing, rates, loading, disc_cols, disc_turb):
    tables = lattice_tables()
    comps, width_x, width_y, depth = populations.shape
    fringe_width = precursor.shape[1]
    turbines = loading.shape[0]
    flat = populations.reshape(comps, width_x * width_y * depth)
    moments = jnp.dot(tables[3], flat, precision=FULL_PRECISION)
    velocity_x = moments[9] / moments[0]
    profile = disc_profile(depth)
    along_y = width_y * lax.axis_size("gy")
    tile_x = lax.axis_index("gx")
    tile_y = lax.axis_index("gy")
    local_x = disc_cols // along_y - tile_x * width_x
    local_y = disc_cols % along_y - tile_y * width_y
    owned = (
        (disc_turb >= 0)
        & (local_x >= 0)
        & (local_x < width_x)
        & (local_y >= 0)
        & (local_y < width_y)
    )
    local_cell = jnp.where(owned, local_x * width_y + local_y, 0)
    columns = velocity_x.reshape(width_x * width_y, depth)[local_cell]
    row_values = jnp.where(owned, jnp.dot(columns, profile, precision=FULL_PRECISION), 0.0)
    owner_table = (disc_turb[None, :] == jnp.arange(turbines, dtype=jnp.int32)[:, None]).astype(
        jnp.float32
    )
    partial_totals = jnp.dot(owner_table, row_values, precision=FULL_PRECISION)
    totals = lax.psum(partial_totals, ("gx", "gy"))
    counts = jnp.sum(owner_table, axis=1)
    disc_speed = totals / (counts * jnp.sum(profile))
    thrust = 0.5 * loading * disc_speed * jnp.abs(disc_speed)
    row_thrust = jnp.dot(thrust, owner_table, precision=FULL_PRECISION)
    placed = (
        (jnp.arange(width_x * width_y, dtype=jnp.int32)[:, None] == local_cell[None, :])
        & owned[None, :]
    ).astype(jnp.float32)
    column_force = jnp.dot(placed, row_thrust, precision=FULL_PRECISION)
    force = -(column_force[:, None] * profile[None, :]).reshape(width_x * width_y * depth)
    post = relax_cells(tables, moments, rates, force).reshape(comps, width_x, width_y, depth)
    source_tile = pairing[tile_x]
    wanted = source_tile * fringe_width + jnp.arange(fringe_width, dtype=jnp.int32)
    piece = lax.all_gather(precursor, "gx", axis=1, tiled=True)
    have = jnp.arange(piece.shape[1], dtype=jnp.int32)
    chosen = (wanted[:, None] == have[None, :]).astype(jnp.float32)
    chosen_pops = jnp.einsum("pr,kryz->kpyz", chosen, piece, precision=FULL_PRECISION)
    selected = jnp.dot(
        tables[5],
        chosen_pops.reshape(comps, fringe_width * width_y * depth),
        precision=FULL_PRECISION,
    )
    rebuilt = jnp.dot(
        tables[6], selected.reshape(10, fringe_width * width_y * depth), precision=FULL_PRECISION
    )
    rebuilt = rebuilt.reshape(comps, fringe_width, width_y, depth)
    blend = (0.5 / (jnp.arange(fringe_width).astype(jnp.float32) + 1.0))[None, :, None, None]
    head = (1.0 - blend) * post[:, :fringe_width] + blend * rebuilt
    post = jnp.concatenate([head, post[:, fringe_width:]], axis=1)
    pieces = []
    padded = extended(post, (("gx", 1), ("gy", 2)), 1)
    for slot in range(27):
        step_x = slot // 9 - 1
        step_y = slot // 3 % 3 - 1
        pieces.append(
            padded[slot, 1 - step_x : 1 - step_x + width_x, 1 - step_y : 1 - step_y + width_y]
        )
    finished = []
    for slot in range(27):
        step_z = slot % 3 - 1
        moved = pieces[slot]
        if step_z == 1:
            moved = jnp.concatenate([post[26 - slot][:, :, :1], moved[:, :, :-1]], axis=2)
        elif step_z == -1:
            moved = jnp.concatenate([moved[:, :, 1:], post[26 - slot][:, :, -1:]], axis=2)
        finished.append(moved)
    return (jnp.stack(finished), disc_speed)


def solution(mesh):
    in_specs = (P(None, "gx", "gy", None), P(None, "gx", "gy", None), P(), P(), P(), P(), P())
    out_specs = (P(None, "gx", "gy", None), P())
    return jax.shard_map(body, mesh=mesh, in_specs=in_specs, out_specs=out_specs, check_vma=False)
```

profile of v0, /device:TPU:0, one launch (start us, length us, event | category | flops | bytes accessed | tf_op | source)
XLA Modules:
  0.0 174.9 jit_solution(11489095928074629085)
XLA Ops:
  7.2 2.2 %copy.22 = f32[27,2,32,128]{3,2,0,1:T(8,128)} copy(f32[27,2,32,128]{3,2,1,0:T(8,128)} %param.15) | data formatting | bytes 1769472 | tf_op args[1]
  9.4 2.4 %pad.213 = f32[32,256,128]{2,1,0:T(8,128)S(1)} pad(f32[27,256,128]{2,1,0:T(8,128)} %bitcast.231, f32[]{:T(128)} %constant.84.clone.1), padding=0_5x0_0x0_0 | pad | bytes 7733252
  11.9 4.5 %copy.26 = f32[4,8,256,128]{3,1,2,0:T(8,128)} copy(f32[4,8,256,128]{3,2,1,0:T(8,128)S(1)} %bitcast.220) | data formatting | bytes 8388608
  16.4 5.4 %fusion.80 = f32[27,32768]{1,0:T(8,128)S(1)} fusion(f32[27,27]{1,0:T(8,128)S(1)} %copy-done.5, f32[27,32768]{1,0:T(8,128)} %bitcast.218), kind=kOutput, calls=%fused_computation.182 | convolution fusion | flops 286654464 | bytes 7080804 | tf_op jit(solution)/shard_map/dot_general | solution.py:112
  21.8 2.1 %copy-done.2 = f32[27,32768]{1,0:T(8,128)} copy-done((f32[27,32768]{1,0:T(8,128)}, f32[27,32768]{1,0:T(8,128)S(1)}, u32[]{:S(2)}) %copy-start.2) | copy-done | bytes 3538968
  23.9 0.5 add_multiply_fusion
  24.5 1.0 gather_fusion
  25.5 0.3 fusion.66
  26.0 43.7 %psum.7 = f32[32]{0:T(128)S(1)} all-reduce(f32[32]{0:T(128)S(1)} %convolution_bitcast_fusion.1), channel_id=1, replica_groups=mesh['gx'=8,'gy'=4] {'gx','gy'}, use_global_device_ids=true, to_apply=%region_0.1 | all-reduce | flops 32 | bytes 256 | tf_op jit(solution)/shard_map/psum | solution.py:134
  69.7 0.6 fusion.73
  70.4 0.7 multiply_divide_fusion
  71.3 0.3 fusion.31
  71.7 7.5 %fusion.1 = f32[27,32768]{1,0:T(8,128)S(1)} fusion(f32[27,32768]{1,0:T(8,128)} %copy-done.2, f32[27,27]{1,0:T(8,128)S(1)} %copy-done.5, f32[32768]{0:T(1024)S(1)} %bitcast.250, f32[32768]{0:T(1024)S(1)} %bitcast.252, f32[27]{0:T(128)S(1)} %copy-done.15, f32[32768]{0:T(1024)S(1)} %bitcast.251, f32[27]{0:T(128)S(1)} %copy-done.16, f32[32768]{0:T(1024)S(1)} %bitcast.217, ...), kind=kOutput, calls=%fused_computation.4 | convolution fusion | flops 299925504 | bytes 7736596 | tf_op jit(solution)/shard_map/dot_general | solution.py:98
  79.3 4.1 %convolution_add_fusion = f32[27,32768]{1,0:T(8,128)S(1)} fusion(f32[27,27]{1,0:T(8,128)S(1)} %copy-done.4, f32[27,32768]{1,0:T(8,128)S(1)} %fusion.1, f32[32768]{0:T(1024)S(1)} %negate_bitcast_fusion, f32[27]{0:T(128)S(1)} %copy-done.10), kind=kOutput, calls=%fused_computation.1 | convolution fusion | flops 288423936 | bytes 7211984 | tf_op jit(solution)/shard_map/dot_general | solution.py:101
  83.5 0.7 copy.27
  84.2 0.4 slice.431
  84.6 1.8 %copy-done = f32[27,256,128]{2,1,0:T(8,128)} copy-done((f32[27,256,128]{2,1,0:T(8,128)}, f32[27,256,128]{2,1,0:T(8,128)S(1)}, u32[]{:S(2)}) %copy-start) | copy-done | bytes 3538968
  86.5 2.6 %collective-permute-start = (f32[27,1,32,128]{3,2,1,0:T(8,128)S(1)}, f32[27,1,32,128]{3,2,1,0:T(8,128)S(1)}, u32[]{:S(2)}, u32[]{:S(2)}) collective-permute-start(f32[27,1,32,128]{3,2,1,0:T(8,128)S(1)} %slice.391), channel_id=1, source_target_pairs={{0,4},{4,8},{8,12},{12,16},{16,20},{20,24},{24,28},{28,0},{1,5},{5... | collective-permute-start | bytes 1327112 | tf_op jit(solution)/shard_map/ppermute | solution.py:17
  89.1 0.6 dynamic_slice.3
  90.2 42.3 %all-gather.2.cloned.1.call-done = f32[27,16,32,128]{3,2,0,1:T(8,128)} async-done(((f32[27,2,32,128]{3,2,0,1:T(8,128)}), f32[27,16,32,128]{3,2,0,1:T(8,128)}) %all-gather.2.cloned.1.call-update) | async-done | bytes 7077904 | tf_op jit(solution)/shard_map/all_gather | solution.py:148
  132.5 9.4 %fusion.26 = f32[27,2,32,128]{3,1,2,0:T(2,128)S(1)} fusion(f32[27,16,32,128]{3,2,0,1:T(8,128)} %all-gather.2.cloned.1.call-done, s32[2]{0:T(128)S(1)} %iota_add_fusion), kind=kOutput, calls=%fused_computation.29 | convolution fusion | flops 42467360 | bytes 7962632 | tf_op jit(solution)/shard_map/pr,kryz->kpyz/dot_general | solution.py:151
  142.2 0.6 copy.28
  142.8 0.7 fusion.81
  143.6 1.0 fusion.82
  144.8 0.3 fusion.29
  145.1 1.4 collective-permute-start.1
  146.5 0.4 slice.393
  146.9 9.8 %collective-permute-done.1 = f32[27,1,32,128]{3,2,1,0:T(8,128)S(1)} collective-permute-done((f32[27,1,32,128]{3,2,1,0:T(8,128)S(1)}, f32[27,1,32,128]{3,2,1,0:T(8,128)S(1)}, u32[]{:S(2)}, u32[]{:S(2)}) %collective-permute-start.1) | collective-permute-done | bytes 442400 | tf_op jit(solution)/shard_map/ppermute | solution.py:19
  156.9 1.7 collective-permute-start.2
  158.7 2.7 %collective-permute-done.3 = f32[27,10,1,128]{3,2,1,0:T(1,128)S(1)} collective-permute-done((f32[27,10,1,128]{3,2,1,0:T(1,128)S(1)}, f32[27,10,1,128]{3,2,1,0:T(1,128)S(1)}, u32[]{:S(2)}, u32[]{:S(2)}) %collective-permute-start.3) | collective-permute-done | bytes 138272 | tf_op jit(solution)/shard_map/ppermute | solution.py:17
  161.4 0.5 collective-permute-done.2
  166.3 1.8 %copy-done.8 = f32[27,8,32,128]{3,2,1,0:T(8,128)} copy-done((f32[27,8,32,128]{3,2,1,0:T(8,128)}, f32[27,8,32,128]{3,2,1,0:T(8,128)S(1)}, u32[]{:S(2)}) %copy-start.8) | copy-done | bytes 3538968
  (100 shorter events, 5.7 us)
Async XLA Ops:
  7.2 125.4 %all-gather.2.cloned.1.call-start = ((), (), s32[]{:S(2)}) async-start(), calls=%async_computation | async-start | bytes 7962624 | tf_op jit(solution)/shard_map/all_gather | solution.py:148
  11.8 4.5 %copy-start.7 = (s32[512]{0:T(512)S(1)}, s32[512]{0:T(512)}, u32[]{:S(2)}) copy-start(s32[512]{0:T(512)} %param.20) | copy-start | bytes 6148
  11.9 4.5 %copy-start.9 = (s32[512]{0:T(512)S(1)}, s32[512]{0:T(512)}, u32[]{:S(2)}) copy-start(s32[512]{0:T(512)} %param.19) | copy-start | bytes 6148
  11.9 4.6 %copy-start.5 = (f32[27,27]{1,0:T(8,128)S(1)}, f32[27,27]{1,0:T(8,128)}, u32[]{:S(2)}) copy-start(f32[27,27]{1,0:T(8,128)} %constant.89.clone) | copy-start | bytes 8752
  21.8 2.1 %copy-start.2 = (f32[27,32768]{1,0:T(8,128)}, f32[27,32768]{1,0:T(8,128)S(1)}, u32[]{:S(2)}) copy-start(f32[27,32768]{1,0:T(8,128)S(1)} %fusion.80) | copy-start | bytes 10616836
  23.9 47.2 %copy-start.12 = (f32[32]{0:T(128)S(1)}, f32[32]{0:T(128)}, u32[]{:S(2)}) copy-start(f32[32]{0:T(128)} %param.18) | copy-start | bytes 388
  23.9 47.7 %copy-start.13 = (f32[27]{0:T(128)S(1)}, f32[27]{0:T(128)}, u32[]{:S(2)}) copy-start(f32[27]{0:T(128)} %param.17) | copy-start | bytes 328
  23.9 47.7 %copy-start.15 = (f32[27]{0:T(128)S(1)}, f32[27]{0:T(128)}, u32[]{:S(2)}) copy-start(f32[27]{0:T(128)} %constant.88.clone) | copy-start | bytes 328
  23.9 47.8 %copy-start.16 = (f32[27]{0:T(128)S(1)}, f32[27]{0:T(128)}, u32[]{:S(2)}) copy-start(f32[27]{0:T(128)} %constant.87.clone) | copy-start | bytes 328
  23.9 47.8 %copy-start.17 = (f32[27]{0:T(128)S(1)}, f32[27]{0:T(128)}, u32[]{:S(2)}) copy-start(f32[27]{0:T(128)} %constant.86.clone) | copy-start | bytes 328
  71.1 8.1 %copy-start.11 = (f32[32]{0:T(128)}, f32[32]{0:T(128)S(1)}, u32[]{:S(2)}) copy-start(f32[32]{0:T(128)S(1)} %multiply_divide_fusion) | copy-start | bytes 388
  71.7 7.7 %copy-start.4 = (f32[27,27]{1,0:T(8,128)S(1)}, f32[27,27]{1,0:T(8,128)}, u32[]{:S(2)}) copy-start(f32[27,27]{1,0:T(8,128)} %constant.90.clone) | copy-start | bytes 8752
  71.7 7.7 %copy-start.10 = (f32[27]{0:T(128)S(1)}, f32[27]{0:T(128)}, u32[]{:S(2)}) copy-start(f32[27]{0:T(128)} %constant.94) | copy-start | bytes 328
  84.2 4.9 %copy-start.14 = (s32[8]{0:T(128)S(1)}, s32[8]{0:T(128)}, u32[]{:S(2)}) copy-start(s32[8]{0:T(128)} %param.16) | copy-start | bytes 100
  84.6 1.8 %copy-start = (f32[27,256,128]{2,1,0:T(8,128)}, f32[27,256,128]{2,1,0:T(8,128)S(1)}, u32[]{:S(2)}) copy-start(f32[27,256,128]{2,1,0:T(8,128)S(1)} %slice.431) | copy-start | bytes 10616836
  86.5 60.4 %collective-permute-start = (f32[27,1,32,128]{3,2,1,0:T(8,128)S(1)}, f32[27,1,32,128]{3,2,1,0:T(8,128)S(1)}, u32[]{:S(2)}, u32[]{:S(2)}) collective-permute-start(f32[27,1,32,128]{3,2,1,0:T(8,128)S(1)} %slice.391), channel_id=1, source_target_pairs={{0,4},{4,8},{8,12},{12,16},{16,20},{20,24},{24,28},{28,0},{1,5},{5... | collective-permute-start | bytes 1327112 | tf_op jit(solution)/shard_map/ppermute | solution.py:17
  141.9 0.9 copy-start.6
  141.9 1.6 copy-start.3
  142.8 2.0 %copy-start.1 = (f32[27,256,128]{2,1,0:T(8,128)S(1)}, f32[27,256,128]{2,1,0:T(8,128)}, u32[]{:S(2)}) copy-start(f32[27,256,128]{2,1,0:T(8,128)} %copy-done) | copy-start | bytes 10616836
  145.1 11.6 %collective-permute-start.1 = (f32[27,1,32,128]{3,2,1,0:T(8,128)S(1)}, f32[27,1,32,128]{3,2,1,0:T(8,128)S(1)}, u32[]{:S(2)}, u32[]{:S(2)}) collective-permute-start(f32[27,1,32,128]{3,2,1,0:T(8,128)S(1)} %slice.394), channel_id=1, source_target_pairs={{4,0},{8,4},{12,8},{16,12},{20,16},{24,20},{28,24},{0,28},{5,1},{9... | collective-permute-start | bytes 1327112 | tf_op jit(solution)/shard_map/ppermute | solution.py:19
  156.9 4.5 %collective-permute-start.3 = (f32[27,10,1,128]{3,2,1,0:T(1,128)S(1)}, f32[27,10,1,128]{3,2,1,0:T(1,128)S(1)}, u32[]{:S(2)}, u32[]{:S(2)}) collective-permute-start(f32[27,10,1,128]{3,2,1,0:T(1,128)S(1)} %get-tuple-element.27), channel_id=1, source_target_pairs={{0,1},{1,2},{2,3},{3,0},{4,5},{5,6},{6,7},{7,4},{8,9},{9,10},{10,1... | collective-permute-start | bytes 414728 | tf_op jit(solution)/shard_map/ppermute | solution.py:17
  156.9 4.9 %collective-permute-start.2 = (f32[27,10,1,128]{3,2,1,0:T(1,128)S(1)}, f32[27,10,1,128]{3,2,1,0:T(1,128)S(1)}, u32[]{:S(2)}, u32[]{:S(2)}) collective-permute-start(f32[27,10,1,128]{3,2,1,0:T(1,128)S(1)} %get-tuple-element.28), channel_id=1, source_target_pairs={{1,0},{2,1},{3,2},{0,3},{5,4},{6,5},{7,6},{4,7},{9,8},{10,9},{11,1... | collective-permute-start | bytes 414728 | tf_op jit(solution)/shard_map/ppermute | solution.py:19
  166.3 1.8 %copy-start.8 = (f32[27,8,32,128]{3,2,1,0:T(8,128)}, f32[27,8,32,128]{3,2,1,0:T(8,128)S(1)}, u32[]{:S(2)}) copy-start(f32[27,8,32,128]{3,2,1,0:T(8,128)S(1)} %fusion.57) | copy-start | bytes 10616836
Sparse Core Ops, SparseCore 0:
  10.2 122.2 all-gather.1
where the time goes:
time: 176 us; the launch traced here: 175 us
  waiting for transfers between devices  55.3 us (31%)
  blocking collectives  43.7 us (25%)
  matrix products  29.1 us (17%)
  local copies, waits for them, and re-layouts  20.8 us (12%)
  between operations  15.3 us (9%)
  starting transfers between devices  5.79 us (3%)
  other arithmetic  4.99 us (3%)
    psum x1, blocking collectives, body(): totals = lax.psum(partial_totals, ('gx', 'gy'))  43.7 us
    all_gather x1, waiting for transfers between devices, body(): piece = lax.all_gather(precursor, 'gx', axis=1, tiled=True)  42.3 us
    unnamed x45, local copies, waits for them, and re-layouts  16.9 us
    ppermute x2, waiting for transfers between devices, extended(): lax.ppermute(head, axis, [((i + 1) % count, i) for i in range(count)])  10.3 us
    dot_general x1, matrix products, body(): jnp.einsum('pr,kryz->kpyz', chosen, piece, precision=FULL_PRECISION)  9.4 us
    dot_general x1, matrix products, relax_cells(): balance_moments = jnp.dot(moment_map, balance, precision=FULL_PRECISION)  7.52 us
    dot_general x1, matrix products, body(): moments = jnp.dot(tables[3], flat, precision=FULL_PRECISION)  5.38 us
    dot_general x1, matrix products, relax_cells(): jnp.dot(back_map, relaxed, precision=FULL_PRECISION)  4.13 us
  transfers between devices with their start and end apart: 5, of which 4 were waited for; matrix products, arithmetic and copies ran while one was open for 24% of the time, Pallas kernels for 0%

commit v1 on v0

v1 whole, which is shorter than its diff:
```python
import functools
import jax
import jax.numpy as jnp
import numpy as np
from jax import lax
from jax.experimental import pallas as pl
from jax.experimental.pallas import tpu as pltpu
from jax.sharding import PartitionSpec as P

MESH = pl.DeviceIdType.MESH
LANES = 128
BLOCK = 8
LOW = (0, 9, 3, 1, 18, 6, 2, 12, 10, 4)


def forward(cells):
    cells = list(cells)
    for stride in (9, 3, 1):
        for i in range(27):
            if (i // stride) % 3 == 0:
                low, mid, high = cells[i], cells[i + stride], cells[i + 2 * stride]
                even = (low + high) * (1.0 / 6.0)
                cells[i] = even + mid * (2.0 / 3.0)
                cells[i + stride] = (high - low) * (1.0 / 6.0)
                cells[i + 2 * stride] = even
    return cells


def backward(moments):
    cells = list(moments)
    for stride in (9, 3, 1):
        for i in range(27):
            if (i // stride) % 3 == 0:
                zero, one, two = cells[i], cells[i + stride], cells[i + 2 * stride]
                odd, even = one * 3.0, two * 3.0
                cells[i] = even - odd
                cells[i + stride] = (zero - two) * 1.5
                cells[i + 2 * stride] = even + odd
    return cells


def balance_moments(density, velocity):
    flux = [density * v for v in velocity]
    out = []
    for i in range(27):
        powers = (i // 9, (i // 3) % 3, i % 3)
        scale = (1.0 / 3.0) ** sum(p == 2 for p in powers)
        odd = [d for d in range(3) if powers[d] == 1]
        if len(odd) == 3:
            out.append(None)
            continue
        if len(odd) == 2:
            value = flux[odd[0]] * velocity[odd[1]]
        elif len(odd) == 1:
            value = flux[odd[0]]
        else:
            value = density
            for d in range(3):
                if powers[d] == 2:
                    value = value + 3.0 * (flux[d] * velocity[d])
        out.append(value if scale == 1.0 else value * scale)
    return out


def rebuild(low):
    rho, jx, jy, jz, xx, yy, zz, xy, xz, yz = low
    base = 2.5 * rho - 1.5 * (xx + yy + zz)
    third = rho * (1.0 / 3.0)
    linear = (3.0 * jx, 3.0 * jy, 3.0 * jz)
    square = (4.5 * (xx - third), 4.5 * (yy - third), 4.5 * (zz - third))
    cross = (9.0 * xy, 9.0 * xz, 9.0 * yz)

    def one(d, step):
        return square[d] + linear[d] if step > 0 else square[d] - linear[d]

    def signed(value, term, sign):
        return value + term if sign > 0 else value - term

    out = []
    for i in range(27):
        steps = (i // 9 - 1, (i // 3) % 3 - 1, i % 3 - 1)
        value = base
        for d in range(3):
            if steps[d]:
                value = value + one(d, steps[d])
        for (a, b), term in zip(((0, 1), (0, 2), (1, 2)), cross):
            if steps[a] * steps[b]:
                value = signed(value, term, steps[a] * steps[b])
        out.append(value)
    return out


def row_of(kx, kz):
    return kx * 3 + kz if kx < 2 else 8 + kz


def kernel(
    n, m, chunk,
    pops_hbm, prec_hbm, pairing, rates, loading, cols, turb,
    out_hbm, speed,
    pops, prec, post, outv, mom, got, stage, final, tot_x, tot_y, load_pad, hits, ysend, yrecv,
    in_sem, out_sem, a_send, a_recv, b_send, b_recv, tx_send, tx_recv, ty_send, ty_recv,
    x_send, x_recv, y_send, y_recv, c_send, c_recv,
):
    comps, width_x, width_y, depth = pops.shape
    fringe = prec.shape[1]
    turbines = loading.shape[1]
    blocks = width_y // BLOCK
    me, my = lax.axis_index("gx"), lax.axis_index("gy")
    right, left = lax.rem(me + 1, n), lax.rem(me + n - 1, n)
    above, below = lax.rem(my + 1, m), lax.rem(my + m - 1, m)

    prec_in = pltpu.make_async_copy(prec_hbm, prec, in_sem.at[0])
    pops_in = pltpu.make_async_copy(pops_hbm, pops, in_sem.at[1])
    prec_in.start()
    pops_in.start()

    barrier = pltpu.get_barrier_semaphore()

    def greet_x(i, _):
        pl.semaphore_signal(barrier, inc=1, device_id={"gx": lax.rem(me + i, n)}, device_id_type=MESH)
        return 0

    def greet_y(i, _):
        pl.semaphore_signal(barrier, inc=1, device_id={"gy": lax.rem(my + i, m)}, device_id_type=MESH)
        return 0

    lax.fori_loop(1, n, greet_x, 0)
    lax.fori_loop(1, m, greet_y, 0)

    heights = lax.broadcasted_iota(jnp.int32, (BLOCK, depth), 1).astype(jnp.float32)
    profile = jnp.exp(-jnp.square((heights - depth / 3.0) / (depth / 6.0)))

    prec_in.wait()
    for p in range(fringe):
        def precursor_block(b, _, p=p):
            rows = pl.ds(pl.multiple_of(b * BLOCK, BLOCK), BLOCK)
            moments = forward([prec[i, p, rows, :] for i in range(27)])
            for q in range(10):
                start = pl.multiple_of((p * 10 + q) * width_y + b * BLOCK, BLOCK)
                mom[pl.ds(start, BLOCK), :] = moments[LOW[q]]
            return 0

        lax.fori_loop(0, blocks, precursor_block, 0)

    pl.semaphore_wait(barrier, n + m - 2)

    def span(j):
        return pl.ds(pl.multiple_of(j * chunk, BLOCK), chunk)

    def first(i):
        to = lax.rem(me + i, n)
        return pltpu.make_async_remote_copy(
            src_ref=mom.at[span(to), :], dst_ref=got.at[me],
            send_sem=a_send.at[to], recv_sem=a_recv.at[me],
            device_id={"gx": to}, device_id_type=MESH)

    def first_in(i):
        source = lax.rem(me + i, n)
        return pltpu.make_async_remote_copy(
            src_ref=mom.at[span(source), :], dst_ref=got.at[source],
            send_sem=a_send.at[source], recv_sem=a_recv.at[source],
            device_id={"gx": source}, device_id_type=MESH)

    def second(i):
        to = lax.rem(me + i, n)
        return pltpu.make_async_remote_copy(
            src_ref=stage.at[to], dst_ref=final.at[span(me), :],
            send_sem=b_send.at[to], recv_sem=b_recv.at[me],
            device_id={"gx": to}, device_id_type=MESH)

    def second_in(i):
        source = lax.rem(me + i, n)
        return pltpu.make_async_remote_copy(
            src_ref=stage.at[source], dst_ref=final.at[span(source), :],
            send_sem=b_send.at[source], recv_sem=b_recv.at[source],
            device_id={"gx": source}, device_id_type=MESH)

    def total_x(i):
        to = lax.rem(me + i, n)
        return pltpu.make_async_remote_copy(
            src_ref=tot_x.at[me], dst_ref=tot_x.at[me],
            send_sem=tx_send.at[to], recv_sem=tx_recv.at[me],
            device_id={"gx": to}, device_id_type=MESH)

    def total_x_in(i):
        source = lax.rem(me + i, n)
        return pltpu.make_async_remote_copy(
            src_ref=tot_x.at[source], dst_ref=tot_x.at[source],
            send_sem=tx_send.at[source], recv_sem=tx_recv.at[source],
            device_id={"gx": source}, device_id_type=MESH)

    def total_y(i):
        to = lax.rem(my + i, m)
        return pltpu.make_async_remote_copy(
            src_ref=tot_y.at[my], dst_ref=tot_y.at[my],
            send_sem=ty_send.at[to], recv_sem=ty_recv.at[my],
            device_id={"gy": to}, device_id_type=MESH)

    def total_y_in(i):
        source = lax.rem(my + i, m)
        return pltpu.make_async_remote_copy(
            src_ref=tot_y.at[source], dst_ref=tot_y.at[source],
            send_sem=ty_send.at[source], recv_sem=ty_recv.at[source],
            device_id={"gy": source}, device_id_type=MESH)

    def each(count, action):
        def step(i, _):
            action(i)
            return 0

        lax.fori_loop(1, count, step, 0)

    each(n, lambda i: first(i).start())

    slots = cols.shape[1]
    owner = (
        lax.broadcasted_iota(jnp.int32, (LANES, slots), 0) == turb[...]
    ).astype(jnp.float32).astype(jnp.bfloat16)
    contract = (((1,), (1,)), ((), ()))
    counts = lax.dot_general(
        jnp.ones((BLOCK, slots), jnp.bfloat16), owner, contract, preferred_element_type=jnp.float32)

    def hit_plane(x, _):
        base = (me * width_x + x) * (width_y * m) + my * width_y
        column = lax.broadcasted_iota(jnp.int32, (width_y, slots), 0) + base
        match = (column == cols[...]).astype(jnp.float32).astype(jnp.bfloat16)
        hits[x] = lax.dot_general(match, owner, contract, preferred_element_type=jnp.float32)
        return 0

    lax.fori_loop(0, width_x, hit_plane, 0)

    pops_in.wait()

    def collide(x, b, acc):
        rows = pl.ds(pl.multiple_of(b * BLOCK, BLOCK), BLOCK)
        moments = forward([pops[i, x, rows, :] for i in range(27)])
        density = moments[0]
        inverse = 1.0 / density
        velocity = [moments[9] * inverse, moments[3] * inverse, moments[1] * inverse]
        row_sum = jnp.sum(velocity[0] * profile, axis=1, keepdims=True)
        acc = acc + row_sum * hits[x, rows, :]
        balance = balance_moments(density, velocity)
        relaxed = []
        for i in range(27):
            gap = moments[i] if balance[i] is None else moments[i] - balance[i]
            relaxed.append(moments[i] - rates[i] * gap)
        for i, value in enumerate(backward(relaxed)):
            post[i, x + 1, rows, :] = value
        return acc

    acc = lax.fori_loop(
        0, width_x,
        lambda x, acc: lax.fori_loop(0, blocks, lambda b, acc: collide(x, b, acc), acc),
        jnp.zeros((BLOCK, LANES), jnp.float32))

    tot_x[me] = jnp.broadcast_to(jnp.sum(acc, axis=0, keepdims=True), (BLOCK, LANES))
    each(n, lambda i: total_x(i).start())

    got[me] = mom[span(me), :]
    each(n, lambda i: first_in(i).wait_recv())

    def forward_chunk(i, _):
        to = lax.rem(me + i, n)
        stage[to] = got[pairing[to]]
        second(i).start()
        return 0

    lax.fori_loop(1, n, forward_chunk, 0)
    final[span(me), :] = got[pairing[me]]

    each(n, lambda i: total_x_in(i).wait_recv())
    tot_y[my] = lax.fori_loop(1, n, lambda i, t: t + tot_x[i], tot_x[0])
    each(m, lambda i: total_y(i).start())
    load_pad[...] = jnp.zeros((BLOCK, LANES), jnp.float32)
    load_pad[:, :turbines] = jnp.broadcast_to(loading[...], (BLOCK, turbines))
    norm = counts * jnp.sum(profile, axis=1, keepdims=True)
    each(m, lambda i: total_y_in(i).wait_recv())
    totals = lax.fori_loop(1, m, lambda i, t: t + tot_y[i], tot_y[0])
    disc_speed = totals / jnp.where(counts > 0.0, norm, 1.0)
    speed[...] = disc_speed[:1, :turbines]
    thrust = (0.5 * load_pad[...] * disc_speed * jnp.abs(disc_speed))[:1]

    def push(x, _):
        column = jnp.sum(hits[x] * thrust, axis=1, keepdims=True)
        kick = (-3.0 * column) * profile[:1]
        for i in range(9):
            post[i, x + 1] = post[i, x + 1] - kick
        for i in range(18, 27):
            post[i, x + 1] = post[i, x + 1] + kick
        return 0

    lax.fori_loop(0, width_x, push, 0)

    def x_copy(way):
        if way:
            src, dst, to = post.at[pl.ds(18, 9), width_x], post.at[pl.ds(18, 9), 0], right
        else:
            src, dst, to = post.at[pl.ds(0, 9), 1], post.at[pl.ds(0, 9), width_x + 1], left
        return pltpu.make_async_remote_copy(
            src_ref=src, dst_ref=dst, send_sem=x_send.at[way], recv_sem=x_recv.at[way],
            device_id={"gx": to}, device_id_type=MESH)

    def y_copy(way, late):
        planes = (0, fringe) if late else (fringe, width_x - fringe)
        return pltpu.make_async_remote_copy(
            src_ref=ysend.at[way, pl.ds(planes[0], planes[1])],
            dst_ref=yrecv.at[way, pl.ds(planes[0] + 1, planes[1])],
            send_sem=y_send.at[2 * way + late], recv_sem=y_recv.at[2 * way + late],
            device_id={"gy": above if way else below}, device_id_type=MESH)

    def corner_copy(way):
        if way:
            src, dst, to = yrecv.at[:, width_x, pl.ds(8, 8)], yrecv.at[:, 0, pl.ds(8, 8)], right
        else:
            src, dst, to = yrecv.at[:, 1, pl.ds(0, 8)], yrecv.at[:, width_x + 1, pl.ds(0, 8)], left
        return pltpu.make_async_remote_copy(
            src_ref=src, dst_ref=dst, send_sem=c_send.at[way], recv_sem=c_recv.at[way],
            device_id={"gx": to}, device_id_type=MESH)

    def pack(x, _):
        for way in range(2):
            edge = width_y - 1 if way else 0
            for kx in range(3):
                for kz in range(3):
                    row = row_of(kx, kz)
                    ysend[way, x, row : row + 1, :] = post[
                        9 * kx + 6 * way + kz, x + 1, edge : edge + 1, :]
        return 0

    lane = lax.broadcasted_iota(jnp.int32, (width_y, depth), 1)
    sub = lax.broadcasted_iota(jnp.int32, (width_y, depth), 0)

    def out_copy(x):
        return pltpu.make_async_copy(outv.at[:, x], out_hbm.at[:, x], out_sem.at[x])

    def stream(x, _):
        for i in range(27):
            kx, ky, kz = i // 9, (i // 3) % 3, i % 3
            source = x + 2 - kx
            moved = post[i, source]
            if ky != 1:
                way = 1 if ky == 2 else 0
                row = row_of(kx, kz)
                halo = yrecv[way, source, row : row + 1, :]
                moved = pltpu.roll(moved, 1 if way else width_y - 1, 0)
                moved = jnp.where(sub == (0 if way else width_y - 1), halo, moved)
            if kz != 1:
                moved = pltpu.roll(moved, 1 if kz == 2 else depth - 1, 1)
                moved = jnp.where(lane == (0 if kz == 2 else depth - 1), post[26 - i, x + 1], moved)
            outv[i, x] = moved
        out_copy(x).start()
        return 0

    x_copy(1).start()
    lax.fori_loop(fringe, width_x, pack, 0)
    for way in range(2):
        y_copy(way, 0).start()
    for way in range(2):
        y_copy(way, 0).wait_recv()
    corner_copy(1).start()
    lax.fori_loop(fringe + 1, width_x - 1, stream, 0)

    each(n, lambda i: second_in(i).wait_recv())
    for p in range(fringe):
        blend = 0.5 / (p + 1.0)

        def blend_block(b, _, p=p, blend=blend):
            rows = pl.ds(pl.multiple_of(b * BLOCK, BLOCK), BLOCK)
            low = []
            for q in range(10):
                start = pl.multiple_of((p * 10 + q) * width_y + b * BLOCK, BLOCK)
                low.append(final[pl.ds(start, BLOCK), :])
            for i, value in enumerate(rebuild(low)):
                post[i, p + 1, rows, :] = (1.0 - blend) * post[i, p + 1, rows, :] + blend * value
            return 0

        lax.fori_loop(0, blocks, blend_block, 0)
        if p == 0:
            x_copy(0).start()

    lax.fori_loop(0, fringe, pack, 0)
    for way in range(2):
        y_copy(way, 1).start()
    for way in range(2):
        y_copy(way, 1).wait_recv()
    corner_copy(0).start()
    x_copy(1).wait_recv()
    corner_copy(1).wait_recv()
    lax.fori_loop(0, fringe + 1, stream, 0)
    x_copy(0).wait_recv()
    corner_copy(0).wait_recv()
    lax.fori_loop(width_x - 1, width_x, stream, 0)

    each(n, lambda i: first(i).wait_send())
    each(n, lambda i: second(i).wait_send())
    each(n, lambda i: total_x(i).wait_send())
    each(m, lambda i: total_y(i).wait_send())
    for way in range(2):
        x_copy(way).wait_send()
        corner_copy(way).wait_send()
        for late in range(2):
            y_copy(way, late).wait_send()

    def drain(x, _):
        out_copy(x).wait()
        return 0

    lax.fori_loop(0, width_x, drain, 0)


def body(n, m, populations, precursor, pairing, rates, loading, disc_cols, disc_turb):
    comps, width_x, width_y, depth = populations.shape
    fringe = precursor.shape[1]
    rows = fringe * 10 * width_y
    chunk = -(-rows // (n * BLOCK)) * BLOCK
    turbines = loading.shape[0]
    slots = disc_cols.shape[0]
    f32 = jnp.float32
    anywhere = pl.BlockSpec(memory_space=pl.ANY)
    smem = pl.BlockSpec(memory_space=pltpu.SMEM)
    vmem = pl.BlockSpec(memory_space=pltpu.VMEM)
    dma = pltpu.SemaphoreType.DMA
    out, speed = pl.pallas_call(
        functools.partial(kernel, n, m, chunk),
        out_shape=(
            jax.ShapeDtypeStruct(populations.shape, f32),
            jax.ShapeDtypeStruct((1, turbines), f32),
        ),
        in_specs=[anywhere, anywhere, smem, smem, vmem, vmem, vmem],
        out_specs=(anywhere, vmem),
        scratch_shapes=[
            pltpu.VMEM(populations.shape, f32),
            pltpu.VMEM(precursor.shape, f32),
            pltpu.VMEM((comps, width_x + 2, width_y, depth), f32),
            pltpu.VMEM(populations.shape, f32),
            pltpu.VMEM((n * chunk, depth), f32),
            pltpu.VMEM((n, chunk, depth), f32),
            pltpu.VMEM((n, chunk, depth), f32),
            pltpu.VMEM((n * chunk, depth), f32),
            pltpu.VMEM((n, BLOCK, LANES), f32),
            pltpu.VMEM((m, BLOCK, LANES), f32),
            pltpu.VMEM((BLOCK, LANES), f32),
            pltpu.VMEM((width_x, width_y, LANES), f32),
            pltpu.VMEM((2, width_x, 16, depth), f32),
            pltpu.VMEM((2, width_x + 2, 16, depth), f32),
            dma((2,)), dma((width_x,)),
            dma((n,)), dma((n,)), dma((n,)), dma((n,)),
            dma((n,)), dma((n,)), dma((m,)), dma((m,)),
            dma((2,)), dma((2,)), dma((4,)), dma((4,)), dma((2,)), dma((2,)),
        ],
        compiler_params=pltpu.CompilerParams(
            collective_id=0, has_side_effects=True, vmem_limit_bytes=40 * 1024 * 1024),
    )(
        populations, precursor, pairing, rates,
        loading.reshape(1, turbines), disc_cols.reshape(1, slots), disc_turb.reshape(1, slots),
    )
    return out, speed.reshape(turbines)


def solution(mesh):
    n, m = mesh.shape["gx"], mesh.shape["gy"]
    in_specs = (P(None, "gx", "gy", None), P(None, "gx", "gy", None), P(), P(), P(), P(), P())
    out_specs = (P(None, "gx", "gy", None), P())
    return jax.shard_map(
        functools.partial(body, n, m), mesh=mesh, in_specs=in_specs, out_specs=out_specs, check_vma=False)
```

time: 176 us -> 42.7 us (0.24)
  waiting for transfers between devices: 55.3 us -> 0 us
  blocking collectives: 43.7 us -> 0 us
  Pallas kernels: 0 us -> 33 us
  matrix products: 29.1 us -> 0 us
  between operations: 15.3 us -> 0.66 us
  local copies, waits for them, and re-layouts: 20.8 us -> 8.79 us
  starting transfers between devices: 5.79 us -> 0 us
  other arithmetic: 4.99 us -> 0 us
    psum x1 -> x0, blocking collectives: 43.7 us -> none  [body(): totals = lax.psum(partial_totals, ('gx', 'gy'))]
    all_gather x1 -> x0, waiting for transfers between devices: 42.3 us -> none  [body(): piece = lax.all_gather(precursor, 'gx', axis=1, tiled=True)]
    pallas_call x0 -> x1, Pallas kernels: none -> 33 us  [body(): pl.pallas_call(functools.partial(kernel, n, m, chunk), out_shape=(jax.Sha...]
    dot_general x10 -> x0, matrix products: 29.1 us -> none  [the longest x1 9.4 us: body(): jnp.einsum('pr,kryz->kpyz', chosen, piece, precision=FULL_PRECISION)]
    ppermute x4 -> x0, waiting for transfers between devices: 13 us -> none  [the longest x2 10.3 us: extended(): lax.ppermute(head, axis, [((i + 1) % count, i) for i in range(count)])]
    unnamed x45 -> x16, local copies, waits for them, and re-layouts: 16.9 us -> 8.79 us
    ppermute x4 -> x0, starting transfers between devices: 5.76 us -> none  [the longest x2 3.08 us: extended(): lax.ppermute(head, axis, [((i + 1) % count, i) for i in range(count)])]
    slice x21 -> x0, local copies, waits for them, and re-layouts: 2.13 us -> none  [the longest x9 0.85 us: body(): post[26 - slot][:, :, -1:]]
  transfers between devices with their start and end apart: 5 -> 0, of which waited for: 4 -> 0; matrix products, arithmetic and copies ran while one was open for 24% -> 0% of each run, Pallas kernels for 0% -> 0%
where the time goes in v1:
time: 42.7 us; the launch traced here: 42.5 us
  Pallas kernels  33 us (77%)
  local copies, waits for them, and re-layouts  8.79 us (21%)
  between operations  0.66 us (2%)
    pallas_call x1, Pallas kernels, body(): pl.pallas_call(functools.partial(kernel, n, m, chunk), out_shape=(jax.Sha...  33 us
    unnamed x16, local copies, waits for them, and re-layouts  8.79 us

profile of v1, /device:TPU:0, one launch (start us, length us, event | category | flops | bytes accessed | tf_op | source)
XLA Modules:
  0.0 42.5 jit_solution(14346732464324064007)
XLA Ops:
  0.6 0.0 copy-start
  0.6 2.0 %copy-done = f32[27,8,32,128]{3,2,1,0:T(8,128)S(1)} copy-done((f32[27,8,32,128]{3,2,1,0:T(8,128)S(1)}, f32[27,8,32,128]{3,2,1,0:T(8,128)}, u32[]{:S(2)}) %copy-start) | copy-done | bytes 3538968
  2.6 0.0 copy-start.1
  2.6 1.2 %copy-done.1 = f32[27,2,32,128]{3,2,1,0:T(8,128)S(1)} copy-done((f32[27,2,32,128]{3,2,1,0:T(8,128)S(1)}, f32[27,2,32,128]{3,2,1,0:T(8,128)}, u32[]{:S(2)}) %copy-start.1) | copy-done | bytes 884760
  3.8 0.0 copy-start.2
  3.8 0.7 %copy-done.2 = s32[512]{0:T(512)S(1)} copy-done((s32[512]{0:T(512)S(1)}, s32[512]{0:T(512)}, u32[]{:S(2)}) %copy-start.2) | copy-done | bytes 2072
  4.5 0.0 copy-start.3
  4.5 0.7 %copy-done.3 = s32[512]{0:T(512)S(1)} copy-done((s32[512]{0:T(512)S(1)}, s32[512]{0:T(512)}, u32[]{:S(2)}) %copy-start.3) | copy-done | bytes 2072
  5.2 0.0 copy-start.4
  5.2 0.7 %copy-done.4 = s32[8]{0:T(128)S(1)} copy-done((s32[8]{0:T(128)S(1)}, s32[8]{0:T(128)}, u32[]{:S(2)}) %copy-start.4) | copy-done | bytes 56
  5.8 0.0 copy-start.5
  5.8 0.7 %copy-done.5 = f32[27]{0:T(128)S(1)} copy-done((f32[27]{0:T(128)S(1)}, f32[27]{0:T(128)}, u32[]{:S(2)}) %copy-start.5) | copy-done | bytes 132
  6.5 0.0 copy-start.6
  6.5 0.7 %copy-done.6 = f32[32]{0:T(128)S(1)} copy-done((f32[32]{0:T(128)S(1)}, f32[32]{0:T(128)}, u32[]{:S(2)}) %copy-start.6) | copy-done | bytes 152
  7.1 33.0 %shard_map.86 = (f32[27,8,32,128]{3,2,1,0:T(8,128)S(1)}, f32[1,32]{1,0:T(1,128)S(1)}) custom-call(f32[27,8,32,128]{3,2,1,0:T(8,128)S(1)} %copy-done, f32[27,2,32,128]{3,2,1,0:T(8,128)S(1)} %copy-done.1, s32[8]{0:T(128)S(1)} %copy-done.4, f32[27]{0:T(128)S(1)} %copy-done.5, f32[1,32]{1,0:T(1,128)S(1)} %bitcast.6, s32[1,512]{1,0:T(1,128)S(1)} %bitcast.4, ...), custom_call_target="tpu_custom_call" | custom-call | tf_op jit(solution)/shard_map/pallas_call | solution.py:424
  40.2 1.8 %copy.11 = f32[27,8,32,128]{3,2,1,0:T(8,128)} copy(f32[27,8,32,128]{3,2,1,0:T(8,128)S(1)} %get-tuple-element.8) | data formatting | bytes 7077888
  42.0 0.5 %copy.12 = f32[32]{0:T(128)} copy(f32[32]{0:T(128)S(1)} %bitcast.7) | data formatting | bytes 256
Async XLA Ops:
  0.6 2.0 %copy-start = (f32[27,8,32,128]{3,2,1,0:T(8,128)S(1)}, f32[27,8,32,128]{3,2,1,0:T(8,128)}, u32[]{:S(2)}) copy-start(f32[27,8,32,128]{3,2,1,0:T(8,128)} %pops_hbm.1) | copy-start | bytes 10616836
  2.6 1.2 %copy-start.1 = (f32[27,2,32,128]{3,2,1,0:T(8,128)S(1)}, f32[27,2,32,128]{3,2,1,0:T(8,128)}, u32[]{:S(2)}) copy-start(f32[27,2,32,128]{3,2,1,0:T(8,128)} %prec_hbm.1) | copy-start | bytes 2654212
  3.8 0.7 %copy-start.2 = (s32[512]{0:T(512)S(1)}, s32[512]{0:T(512)}, u32[]{:S(2)}) copy-start(s32[512]{0:T(512)} %param.12) | copy-start | bytes 6148
  4.5 0.7 %copy-start.3 = (s32[512]{0:T(512)S(1)}, s32[512]{0:T(512)}, u32[]{:S(2)}) copy-start(s32[512]{0:T(512)} %param.13) | copy-start | bytes 6148
  5.2 0.7 %copy-start.4 = (s32[8]{0:T(128)S(1)}, s32[8]{0:T(128)}, u32[]{:S(2)}) copy-start(s32[8]{0:T(128)} %pairing.1) | copy-start | bytes 100
  5.8 0.7 %copy-start.5 = (f32[27]{0:T(128)S(1)}, f32[27]{0:T(128)}, u32[]{:S(2)}) copy-start(f32[27]{0:T(128)} %rates.1) | copy-start | bytes 328
  6.5 0.7 %copy-start.6 = (f32[32]{0:T(128)S(1)}, f32[32]{0:T(128)}, u32[]{:S(2)}) copy-start(f32[32]{0:T(128)} %param.11) | copy-start | bytes 388

commit v2 on v1

--- a/solution.py
+++ b/solution.py
@@ -96,11 +96,12 @@
 
 def kernel(
     n, m, chunk,
-    pops_hbm, prec_hbm, pairing, rates, loading, cols, turb,
+    pops_hbm, prec_hbm, pairing_hbm, rates_hbm, loading_hbm, cols_hbm, turb_hbm,
     out_hbm, speed,
-    pops, prec, post, outv, mom, got, stage, final, tot_x, tot_y, load_pad, hits, ysend, yrecv,
+    pops, prec, pairing, rates, loading, cols, turb,
+    post, outv, mom, stage, final, tot_x, tot_y, load_pad, hits, ysend, yrecv,
     in_sem, out_sem, a_send, a_recv, b_send, b_recv, tx_send, tx_recv, ty_send, ty_recv,
-    x_send, x_recv, y_send, y_recv, c_send, c_recv,
+    x_send, x_recv, y_send, y_recv, c_send, c_recv, *got,
 ):
     comps, width_x, width_y, depth = pops.shape
     fringe = prec.shape[1]
@@ -110,10 +111,16 @@
     right, left = lax.rem(me + 1, n), lax.rem(me + n - 1, n)
     above, below = lax.rem(my + 1, m), lax.rem(my + m - 1, m)
 
-    prec_in = pltpu.make_async_copy(prec_hbm, prec, in_sem.at[0])
-    pops_in = pltpu.make_async_copy(pops_hbm, pops, in_sem.at[1])
-    prec_in.start()
-    pops_in.start()
+    prec_in = [
+        pltpu.make_async_copy(prec_hbm.at[:, p], prec.at[:, p], in_sem.at[p]) for p in range(fringe)]
+    small_in = [
+        pltpu.make_async_copy(source, target, in_sem.at[fringe + 1 + k])
+        for k, (source, target) in enumerate((
+            (cols_hbm, cols), (turb_hbm, turb), (pairing_hbm, pairing), (rates_hbm, rates),
+            (loading_hbm, loading)))]
+    pops_in = pltpu.make_async_copy(pops_hbm, pops, in_sem.at[fringe])
+    for copy in prec_in + small_in + [pops_in]:
+        copy.start()
 
     barrier = pltpu.get_barrier_semaphore()
 
@@ -131,88 +138,66 @@
     heights = lax.broadcasted_iota(jnp.int32, (BLOCK, depth), 1).astype(jnp.float32)
     profile = jnp.exp(-jnp.square((heights - depth / 3.0) / (depth / 6.0)))
 
-    prec_in.wait()
+    def span(j):
+        return pl.ds(pl.multiple_of(j * chunk, BLOCK), chunk)
+
+    def first(p, i, sent):
+        other = lax.rem(me + i, n)
+        slot = me if sent else other
+        return pltpu.make_async_remote_copy(
+            src_ref=mom.at[p, span(other), :], dst_ref=got[p].at[slot],
+            send_sem=a_send.at[p * n + other], recv_sem=a_recv.at[p * n + slot],
+            device_id={"gx": other}, device_id_type=MESH)
+
+    def second(p, i, sent):
+        other = lax.rem(me + i, n)
+        slot = me if sent else other
+        return pltpu.make_async_remote_copy(
+            src_ref=stage.at[p, other], dst_ref=final.at[p, span(slot), :],
+            send_sem=b_send.at[p * n + other], recv_sem=b_recv.at[p * n + slot],
+            device_id={"gx": other}, device_id_type=MESH)
+
+    def total_x(i, sent):
+        other = lax.rem(me + i, n)
+        slot = me if sent else other
+        return pltpu.make_async_remote_copy(
+            src_ref=tot_x.at[slot], dst_ref=tot_x.at[slot],
+            send_sem=tx_send.at[other], recv_sem=tx_recv.at[slot],
+            device_id={"gx": other}, device_id_type=MESH)
+
+    def total_y(i, sent):
+        other = lax.rem(my + i, m)
+        slot = my if sent else other
+        return pltpu.make_async_remote_copy(
+            src_ref=tot_y.at[slot], dst_ref=tot_y.at[slot],
+            send_sem=ty_send.at[other], recv_sem=ty_recv.at[slot],
+            device_id={"gy": other}, device_id_type=MESH)
+
+    def each(count, action):
+        def step(i, _):
+            action(i)
+            return 0
+
+        lax.fori_loop(1, count, step, 0)
+
     for p in range(fringe):
+        prec_in[p].wait()
+
         def precursor_block(b, _, p=p):
             rows = pl.ds(pl.multiple_of(b * BLOCK, BLOCK), BLOCK)
             moments = forward([prec[i, p, rows, :] for i in range(27)])
             for q in range(10):
-                start = pl.multiple_of((p * 10 + q) * width_y + b * BLOCK, BLOCK)
-                mom[pl.ds(start, BLOCK), :] = moments[LOW[q]]
+                start = pl.multiple_of(q * width_y + b * BLOCK, BLOCK)
+                mom[p, pl.ds(start, BLOCK), :] = moments[LOW[q]]
             return 0
 
         lax.fori_loop(0, blocks, precursor_block, 0)
-
-    pl.semaphore_wait(barrier, n + m - 2)
-
-    def span(j):
-        return pl.ds(pl.multiple_of(j * chunk, BLOCK), chunk)
-
-    def first(i):
-        to = lax.rem(me + i, n)
-        return pltpu.make_async_remote_copy(
-            src_ref=mom.at[span(to), :], dst_ref=got.at[me],
-            send_sem=a_send.at[to], recv_sem=a_recv.at[me],
-            device_id={"gx": to}, device_id_type=MESH)
-
-    def first_in(i):
-        source = lax.rem(me + i, n)
-        return pltpu.make_async_remote_copy(
-            src_ref=mom.at[span(source), :], dst_ref=got.at[source],
-            send_sem=a_send.at[source], recv_sem=a_recv.at[source],
-            device_id={"gx": source}, device_id_type=MESH)
-
-    def second(i):
-        to = lax.rem(me + i, n)
-        return pltpu.make_async_remote_copy(
-            src_ref=stage.at[to], dst_ref=final.at[span(me), :],
-            send_sem=b_send.at[to], recv_sem=b_recv.at[me],
-            device_id={"gx": to}, device_id_type=MESH)
-
-    def second_in(i):
-        source = lax.rem(me + i, n)
-        return pltpu.make_async_remote_copy(
-            src_ref=stage.at[source], dst_ref=final.at[span(source), :],
-            send_sem=b_send.at[source], recv_sem=b_recv.at[source],
-            device_id={"gx": source}, device_id_type=MESH)
-
-    def total_x(i):
-        to = lax.rem(me + i, n)
-        return pltpu.make_async_remote_copy(
-            src_ref=tot_x.at[me], dst_ref=tot_x.at[me],
-            send_sem=tx_send.at[to], recv_sem=tx_recv.at[me],
-            device_id={"gx": to}, device_id_type=MESH)
-
-    def total_x_in(i):
-        source = lax.rem(me + i, n)
-        return pltpu.make_async_remote_copy(
-            src_ref=tot_x.at[source], dst_ref=tot_x.at[source],
-            send_sem=tx_send.at[source], recv_sem=tx_recv.at[source],
-            device_id={"gx": source}, device_id_type=MESH)
-
-    def total_y(i):
-        to = lax.rem(my + i, m)
-        return pltpu.make_async_remote_copy(
-            src_ref=tot_y.at[my], dst_ref=tot_y.at[my],
-            send_sem=ty_send.at[to], recv_sem=ty_recv.at[my],
-            device_id={"gy": to}, device_id_type=MESH)
-
-    def total_y_in(i):
-        source = lax.rem(my + i, m)
-        return pltpu.make_async_remote_copy(
-            src_ref=tot_y.at[source], dst_ref=tot_y.at[source],
-            send_sem=ty_send.at[source], recv_sem=ty_recv.at[source],
-            device_id={"gy": source}, device_id_type=MESH)
-
-    def each(count, action):
-        def step(i, _):
-            action(i)
-            return 0
-
-        lax.fori_loop(1, count, step, 0)
-
-    each(n, lambda i: first(i).start())
-
+        if p == 0:
+            pl.semaphore_wait(barrier, n + m - 2)
+        each(n, lambda i, p=p: first(p, i, True).start())
+
+    for copy in small_in:
+        copy.wait()
     slots = cols.shape[1]
     owner = (
         lax.broadcasted_iota(jnp.int32, (LANES, slots), 0) == turb[...]
@@ -220,26 +205,38 @@
     contract = (((1,), (1,)), ((), ()))
     counts = lax.dot_general(
         jnp.ones((BLOCK, slots), jnp.bfloat16), owner, contract, preferred_element_type=jnp.float32)
-
-    def hit_plane(x, _):
-        base = (me * width_x + x) * (width_y * m) + my * width_y
-        column = lax.broadcasted_iota(jnp.int32, (width_y, slots), 0) + base
-        match = (column == cols[...]).astype(jnp.float32).astype(jnp.bfloat16)
-        hits[x] = lax.dot_general(match, owner, contract, preferred_element_type=jnp.float32)
-        return 0
-
-    lax.fori_loop(0, width_x, hit_plane, 0)
+    shape = (width_x, width_y, slots)
+    column = (
+        (lax.broadcasted_iota(jnp.int32, shape, 0) + me * width_x) * (width_y * m)
+        + lax.broadcasted_iota(jnp.int32, shape, 1) + my * width_y)
+    match = (column == cols[...].reshape(1, 1, slots)).astype(jnp.float32).astype(jnp.bfloat16)
+    hits[...] = lax.dot_general(
+        match.reshape(width_x * width_y, slots), owner, contract, preferred_element_type=jnp.float32
+    ).reshape(width_x, width_y, LANES)
 
     pops_in.wait()
 
-    def collide(x, b, acc):
+    def share(x, acc):
+        sheets = []
+        for kx in range(3):
+            c = [pops[9 * kx + k, x] for k in range(9)]
+            corner = (c[0] + c[2]) + (c[6] + c[8])
+            edge = (c[1] + c[3]) + (c[5] + c[7])
+            sheets.append(corner * (1.0 / 36.0) + edge * (1.0 / 9.0) + c[4] * (4.0 / 9.0))
+        density = (sheets[0] + sheets[2]) * (1.0 / 6.0) + sheets[1] * (2.0 / 3.0)
+        velocity = (sheets[2] - sheets[0]) * (1.0 / 6.0) / density
+        return acc + jnp.sum(velocity * profile[:1], axis=1, keepdims=True) * hits[x]
+
+    acc = lax.fori_loop(0, width_x, share, jnp.zeros((width_y, LANES), jnp.float32))
+    tot_x[me] = jnp.broadcast_to(jnp.sum(acc, axis=0, keepdims=True), (BLOCK, LANES))
+    each(n, lambda i: total_x(i, True).start())
+
+    def collide_block(x, b):
         rows = pl.ds(pl.multiple_of(b * BLOCK, BLOCK), BLOCK)
         moments = forward([pops[i, x, rows, :] for i in range(27)])
         density = moments[0]
         inverse = 1.0 / density
         velocity = [moments[9] * inverse, moments[3] * inverse, moments[1] * inverse]
-        row_sum = jnp.sum(velocity[0] * profile, axis=1, keepdims=True)
-        acc = acc + row_sum * hits[x, rows, :]
         balance = balance_moments(density, velocity)
         relaxed = []
         for i in range(27):
@@ -247,35 +244,41 @@
             relaxed.append(moments[i] - rates[i] * gap)
         for i, value in enumerate(backward(relaxed)):
             post[i, x + 1, rows, :] = value
-        return acc
-
-    acc = lax.fori_loop(
-        0, width_x,
-        lambda x, acc: lax.fori_loop(0, blocks, lambda b, acc: collide(x, b, acc), acc),
-        jnp.zeros((BLOCK, LANES), jnp.float32))
-
-    tot_x[me] = jnp.broadcast_to(jnp.sum(acc, axis=0, keepdims=True), (BLOCK, LANES))
-    each(n, lambda i: total_x(i).start())
-
-    got[me] = mom[span(me), :]
-    each(n, lambda i: first_in(i).wait_recv())
-
-    def forward_chunk(i, _):
-        to = lax.rem(me + i, n)
-        stage[to] = got[pairing[to]]
-        second(i).start()
-        return 0
-
-    lax.fori_loop(1, n, forward_chunk, 0)
-    final[span(me), :] = got[pairing[me]]
-
-    each(n, lambda i: total_x_in(i).wait_recv())
+
+    def collide(start, stop):
+        def step(k, _):
+            collide_block(k // blocks, k % blocks)
+            return 0
+
+        lax.fori_loop(start * blocks, stop * blocks, step, 0)
+
+    def pass_on(p):
+        got[p][me] = mom[p, span(me), :]
+        each(n, lambda i: first(p, i, False).wait_recv())
+
+        def forward_chunk(i, _):
+            to = lax.rem(me + i, n)
+            stage[p, to] = got[p][pairing[to]]
+            second(p, i, True).start()
+            return 0
+
+        lax.fori_loop(1, n, forward_chunk, 0)
+        final[p, span(me), :] = got[p][pairing[me]]
+
+    part = -(-width_x // (fringe + 1))
+    for p in range(fringe):
+        collide(p * part, (p + 1) * part)
+        pass_on(p)
+
+    each(n, lambda i: total_x(i, False).wait_recv())
     tot_y[my] = lax.fori_loop(1, n, lambda i, t: t + tot_x[i], tot_x[0])
-    each(m, lambda i: total_y(i).start())
+    each(m, lambda i: total_y(i, True).start())
+    collide(fringe * part, width_x)
+
     load_pad[...] = jnp.zeros((BLOCK, LANES), jnp.float32)
     load_pad[:, :turbines] = jnp.broadcast_to(loading[...], (BLOCK, turbines))
     norm = counts * jnp.sum(profile, axis=1, keepdims=True)
-    each(m, lambda i: total_y_in(i).wait_recv())
+    each(m, lambda i: total_y(i, False).wait_recv())
     totals = lax.fori_loop(1, m, lambda i, t: t + tot_y[i], tot_y[0])
     disc_speed = totals / jnp.where(counts > 0.0, norm, 1.0)
     speed[...] = disc_speed[:1, :turbines]
@@ -356,21 +359,17 @@
     lax.fori_loop(fringe, width_x, pack, 0)
     for way in range(2):
         y_copy(way, 0).start()
-    for way in range(2):
-        y_copy(way, 0).wait_recv()
-    corner_copy(1).start()
-    lax.fori_loop(fringe + 1, width_x - 1, stream, 0)
-
-    each(n, lambda i: second_in(i).wait_recv())
+
     for p in range(fringe):
         blend = 0.5 / (p + 1.0)
+        each(n, lambda i, p=p: second(p, i, False).wait_recv())
 
         def blend_block(b, _, p=p, blend=blend):
             rows = pl.ds(pl.multiple_of(b * BLOCK, BLOCK), BLOCK)
             low = []
             for q in range(10):
-                start = pl.multiple_of((p * 10 + q) * width_y + b * BLOCK, BLOCK)
-                low.append(final[pl.ds(start, BLOCK), :])
+                start = pl.multiple_of(q * width_y + b * BLOCK, BLOCK)
+                low.append(final[p, pl.ds(start, BLOCK), :])
             for i, value in enumerate(rebuild(low)):
                 post[i, p + 1, rows, :] = (1.0 - blend) * post[i, p + 1, rows, :] + blend * value
             return 0
@@ -383,8 +382,12 @@
     for way in range(2):
         y_copy(way, 1).start()
     for way in range(2):
+        y_copy(way, 0).wait_recv()
+    corner_copy(1).start()
+    for way in range(2):
         y_copy(way, 1).wait_recv()
     corner_copy(0).start()
+    lax.fori_loop(fringe + 1, width_x - 1, stream, 0)
     x_copy(1).wait_recv()
     corner_copy(1).wait_recv()
     lax.fori_loop(0, fringe + 1, stream, 0)
@@ -392,10 +395,11 @@
     corner_copy(0).wait_recv()
     lax.fori_loop(width_x - 1, width_x, stream, 0)
 
-    each(n, lambda i: first(i).wait_send())
-    each(n, lambda i: second(i).wait_send())
-    each(n, lambda i: total_x(i).wait_send())
-    each(m, lambda i: total_y(i).wait_send())
+    for p in range(fringe):
+        each(n, lambda i, p=p: first(p, i, True).wait_send())
+        each(n, lambda i, p=p: second(p, i, True).wait_send())
+    each(n, lambda i: total_x(i, True).wait_send())
+    each(m, lambda i: total_y(i, True).wait_send())
     for way in range(2):
         x_copy(way).wait_send()
         corner_copy(way).wait_send()
@@ -412,13 +416,13 @@
 def body(n, m, populations, precursor, pairing, rates, loading, disc_cols, disc_turb):
     comps, width_x, width_y, depth = populations.shape
     fringe = precursor.shape[1]
-    rows = fringe * 10 * width_y
+    rows = 10 * width_y
     chunk = -(-rows // (n * BLOCK)) * BLOCK
     turbines = loading.shape[0]
     slots = disc_cols.shape[0]
     f32 = jnp.float32
     anywhere = pl.BlockSpec(memory_space=pl.ANY)
-    smem = pl.BlockSpec(memory_space=pltpu.SMEM)
+    hbm = pl.BlockSpec(memory_space=pltpu.HBM)
     vmem = pl.BlockSpec(memory_space=pltpu.VMEM)
     dma = pltpu.SemaphoreType.DMA
     out, speed = pl.pallas_call(
@@ -427,30 +431,34 @@
             jax.ShapeDtypeStruct(populations.shape, f32),
             jax.ShapeDtypeStruct((1, turbines), f32),
         ),
-        in_specs=[anywhere, anywhere, smem, smem, vmem, vmem, vmem],
+        in_specs=[hbm] * 7,
         out_specs=(anywhere, vmem),
         scratch_shapes=[
             pltpu.VMEM(populations.shape, f32),
             pltpu.VMEM(precursor.shape, f32),
+            pltpu.SMEM(pairing.shape, jnp.int32),
+            pltpu.SMEM(rates.shape, f32),
+            pltpu.VMEM((1, turbines), f32),
+            pltpu.VMEM((1, slots), jnp.int32),
+            pltpu.VMEM((1, slots), jnp.int32),
             pltpu.VMEM((comps, width_x + 2, width_y, depth), f32),
             pltpu.VMEM(populations.shape, f32),
-            pltpu.VMEM((n * chunk, depth), f32),
-            pltpu.VMEM((n, chunk, depth), f32),
-            pltpu.VMEM((n, chunk, depth), f32),
-            pltpu.VMEM((n * chunk, depth), f32),
+            pltpu.VMEM((fringe, n * chunk, depth), f32),
+            pltpu.VMEM((fringe, n, chunk, depth), f32),
+            pltpu.VMEM((fringe, n * chunk, depth), f32),
             pltpu.VMEM((n, BLOCK, LANES), f32),
             pltpu.VMEM((m, BLOCK, LANES), f32),
             pltpu.VMEM((BLOCK, LANES), f32),
             pltpu.VMEM((width_x, width_y, LANES), f32),
             pltpu.VMEM((2, width_x, 16, depth), f32),
             pltpu.VMEM((2, width_x + 2, 16, depth), f32),
-            dma((2,)), dma((width_x,)),
-            dma((n,)), dma((n,)), dma((n,)), dma((n,)),
+            dma((fringe + 6,)), dma((width_x,)),
+            dma((fringe * n,)), dma((fringe * n,)), dma((fringe * n,)), dma((fringe * n,)),
             dma((n,)), dma((n,)), dma((m,)), dma((m,)),
             dma((2,)), dma((2,)), dma((4,)), dma((4,)), dma((2,)), dma((2,)),
-        ],
+        ] + [pltpu.VMEM((n, chunk, depth), f32)] * fringe,
         compiler_params=pltpu.CompilerParams(
-            collective_id=0, has_side_effects=True, vmem_limit_bytes=40 * 1024 * 1024),
+            collective_id=0, has_side_effects=True, vmem_limit_bytes=64 * 1024 * 1024),
     )(
         populations, precursor, pairing, rates,
         loading.reshape(1, turbines), disc_cols.reshape(1, slots), disc_turb.reshape(1, slots),

time: 42.7 us -> 39.8 us (0.932)
  local copies, waits for them, and re-layouts: 8.79 us -> 4.9 us
  Pallas kernels: 33 us -> 34.1 us
    unnamed x16 -> x4, local copies, waits for them, and re-layouts: 8.79 us -> 4.9 us
    pallas_call x1, Pallas kernels: 33 us -> 34.1 us  [body(): pl.pallas_call(functools.partial(kernel, n, m, chunk), out_shape=(jax.Sha...]
where the time goes in v2:
time: 39.8 us; the launch traced here: 39.7 us
  Pallas kernels  34.1 us (86%)
  local copies, waits for them, and re-layouts  4.9 us (12%)
  between operations  0.65 us (2%)
    pallas_call x1, Pallas kernels, body(): pl.pallas_call(functools.partial(kernel, n, m, chunk), out_shape=(jax.Sha...  34.1 us
    unnamed x4, local copies, waits for them, and re-layouts  4.9 us

profile of v2, /device:TPU:0, one launch (start us, length us, event | category | flops | bytes accessed | tf_op | source)
XLA Modules:
  0.0 39.7 jit_solution(2343755638112458050)
XLA Ops:
  0.6 34.1 %shard_map.86 = (f32[27,8,32,128]{3,2,1,0:T(8,128)}, f32[1,32]{1,0:T(1,128)}) custom-call(f32[27,8,32,128]{3,2,1,0:T(8,128)} %pops_hbm.1, f32[27,2,32,128]{3,2,1,0:T(8,128)} %prec_hbm.1, s32[8]{0:T(128)} %pairing_hbm.1, f32[27]{0:T(128)} %rates_hbm.1, f32[1,32]{1,0:T(1,128)} %bitcast.6, s32[1,512]{1,0:T(1,128)} %bitcast.4, s32[1,512]{1,0:T(1,128)} %bitcast.5), custom_call_target="tpu_custom_call" | custom-call | tf_op jit(solution)/shard_map/pallas_call | solution.py:428
  34.7 0.0 copy-start
  34.7 4.4 %copy.11 = f32[27,8,32,128]{3,2,1,0:T(8,128)} copy(f32[27,8,32,128]{3,2,1,0:T(8,128)} %get-tuple-element.8) | data formatting | bytes 7077888
  39.1 0.0 copy-done
  39.1 0.5 %copy.12 = f32[32]{0:T(128)} copy(f32[32]{0:T(128)S(1)} %bitcast.7) | data formatting | bytes 256
Async XLA Ops:
  34.7 4.4 %copy-start = (f32[1,32]{1,0:T(1,128)S(1)}, f32[1,32]{1,0:T(1,128)}, u32[]{:S(2)}) copy-start(f32[1,32]{1,0:T(1,128)} %get-tuple-element.5) | copy-start | bytes 388

commit v3 on v2

--- a/solution.py
+++ b/solution.py
@@ -97,10 +97,10 @@
 def kernel(
     n, m, chunk,
     pops_hbm, prec_hbm, pairing_hbm, rates_hbm, loading_hbm, cols_hbm, turb_hbm,
-    out_hbm, speed,
+    out, speed,
     pops, prec, pairing, rates, loading, cols, turb,
-    post, outv, mom, stage, final, tot_x, tot_y, load_pad, hits, ysend, yrecv,
-    in_sem, out_sem, a_send, a_recv, b_send, b_recv, tx_send, tx_recv, ty_send, ty_recv,
+    post, mom, stage, final, tot_x, tot_y, load_pad, hits, ysend, yrecv,
+    in_sem, a_send, a_recv, b_send, b_recv, tx_send, tx_recv, ty_send, ty_recv,
     x_send, x_recv, y_send, y_recv, c_send, c_recv, *got,
 ):
     comps, width_x, width_y, depth = pops.shape
@@ -141,21 +141,27 @@
     def span(j):
         return pl.ds(pl.multiple_of(j * chunk, BLOCK), chunk)
 
+    half = n // 2
+    group, place = me // half, lax.rem(me, half)
+
+    def partner(i):
+        return lax.rem(group + 1 + i // half, 2) * half + lax.rem(place + i, half)
+
     def first(p, i, sent):
-        other = lax.rem(me + i, n)
+        other = partner(i)
         slot = me if sent else other
         return pltpu.make_async_remote_copy(
-            src_ref=mom.at[p, span(other), :], dst_ref=got[p].at[slot],
+            src_ref=mom.at[p, span(lax.rem(other, half)), :], dst_ref=got[p].at[slot],
             send_sem=a_send.at[p * n + other], recv_sem=a_recv.at[p * n + slot],
             device_id={"gx": other}, device_id_type=MESH)
 
     def second(p, i, sent):
-        other = lax.rem(me + i, n)
-        slot = me if sent else other
+        other = lax.rem(place + i, half)
+        slot = place if sent else other
         return pltpu.make_async_remote_copy(
             src_ref=stage.at[p, other], dst_ref=final.at[p, span(slot), :],
-            send_sem=b_send.at[p * n + other], recv_sem=b_recv.at[p * n + slot],
-            device_id={"gx": other}, device_id_type=MESH)
+            send_sem=b_send.at[p * half + other], recv_sem=b_recv.at[p * half + slot],
+            device_id={"gx": group * half + other}, device_id_type=MESH)
 
     def total_x(i, sent):
         other = lax.rem(me + i, n)
@@ -179,6 +185,14 @@
             return 0
 
         lax.fori_loop(1, count, step, 0)
+
+    def partners(action):
+        def step(i, _):
+            action(i)
+            return 0
+
+        lax.fori_loop(0, half, step, 0)
+        lax.fori_loop(half + 1, n, step, 0)
 
     for p in range(fringe):
         prec_in[p].wait()
@@ -194,7 +208,7 @@
         lax.fori_loop(0, blocks, precursor_block, 0)
         if p == 0:
             pl.semaphore_wait(barrier, n + m - 2)
-        each(n, lambda i, p=p: first(p, i, True).start())
+        partners(lambda i, p=p: first(p, i, True).start())
 
     for copy in small_in:
         copy.wait()
@@ -253,17 +267,17 @@
         lax.fori_loop(start * blocks, stop * blocks, step, 0)
 
     def pass_on(p):
-        got[p][me] = mom[p, span(me), :]
-        each(n, lambda i: first(p, i, False).wait_recv())
+        got[p][me] = mom[p, span(place), :]
+        partners(lambda i: first(p, i, False).wait_recv())
 
         def forward_chunk(i, _):
-            to = lax.rem(me + i, n)
-            stage[p, to] = got[p][pairing[to]]
+            to = lax.rem(place + i, half)
+            stage[p, to] = got[p][pairing[group * half + to]]
             second(p, i, True).start()
             return 0
 
-        lax.fori_loop(1, n, forward_chunk, 0)
-        final[p, span(me), :] = got[p][pairing[me]]
+        lax.fori_loop(1, half, forward_chunk, 0)
+        final[p, span(place), :] = got[p][pairing[me]]
 
     part = -(-width_x // (fringe + 1))
     for p in range(fringe):
@@ -305,11 +319,11 @@
             device_id={"gx": to}, device_id_type=MESH)
 
     def y_copy(way, late):
-        planes = (0, fringe) if late else (fringe, width_x - fringe)
+        planes = (late - 1, 1) if late else (fringe, width_x - fringe)
         return pltpu.make_async_remote_copy(
             src_ref=ysend.at[way, pl.ds(planes[0], planes[1])],
             dst_ref=yrecv.at[way, pl.ds(planes[0] + 1, planes[1])],
-            send_sem=y_send.at[2 * way + late], recv_sem=y_recv.at[2 * way + late],
+            send_sem=y_send.at[(fringe + 1) * way + late], recv_sem=y_recv.at[(fringe + 1) * way + late],
             device_id={"gy": above if way else below}, device_id_type=MESH)
 
     def corner_copy(way):
@@ -333,9 +347,6 @@
 
     lane = lax.broadcasted_iota(jnp.int32, (width_y, depth), 1)
     sub = lax.broadcasted_iota(jnp.int32, (width_y, depth), 0)
-
-    def out_copy(x):
-        return pltpu.make_async_copy(outv.at[:, x], out_hbm.at[:, x], out_sem.at[x])
 
     def stream(x, _):
         for i in range(27):
@@ -351,8 +362,7 @@
             if kz != 1:
                 moved = pltpu.roll(moved, 1 if kz == 2 else depth - 1, 1)
                 moved = jnp.where(lane == (0 if kz == 2 else depth - 1), post[26 - i, x + 1], moved)
-            outv[i, x] = moved
-        out_copy(x).start()
+            out[i, x] = moved
         return 0
 
     x_copy(1).start()
@@ -362,7 +372,7 @@
 
     for p in range(fringe):
         blend = 0.5 / (p + 1.0)
-        each(n, lambda i, p=p: second(p, i, False).wait_recv())
+        each(half, lambda i, p=p: second(p, i, False).wait_recv())
 
         def blend_block(b, _, p=p, blend=blend):
             rows = pl.ds(pl.multiple_of(b * BLOCK, BLOCK), BLOCK)
@@ -377,17 +387,21 @@
         lax.fori_loop(0, blocks, blend_block, 0)
         if p == 0:
             x_copy(0).start()
-
-    lax.fori_loop(0, fringe, pack, 0)
-    for way in range(2):
-        y_copy(way, 1).start()
-    for way in range(2):
-        y_copy(way, 0).wait_recv()
-    corner_copy(1).start()
+        pack(p, 0)
+        for way in range(2):
+            y_copy(way, p + 1).start()
+        if p == 0:
+            for way in range(2):
+                y_copy(way, 0).wait_recv()
+            corner_copy(1).start()
+
     for way in range(2):
         y_copy(way, 1).wait_recv()
     corner_copy(0).start()
     lax.fori_loop(fringe + 1, width_x - 1, stream, 0)
+    for late in range(2, fringe + 1):
+        for way in range(2):
+            y_copy(way, late).wait_recv()
     x_copy(1).wait_recv()
     corner_copy(1).wait_recv()
     lax.fori_loop(0, fringe + 1, stream, 0)
@@ -396,43 +410,37 @@
     lax.fori_loop(width_x - 1, width_x, stream, 0)
 
     for p in range(fringe):
-        each(n, lambda i, p=p: first(p, i, True).wait_send())
-        each(n, lambda i, p=p: second(p, i, True).wait_send())
+        partners(lambda i, p=p: first(p, i, True).wait_send())
+        each(half, lambda i, p=p: second(p, i, True).wait_send())
     each(n, lambda i: total_x(i, True).wait_send())
     each(m, lambda i: total_y(i, True).wait_send())
     for way in range(2):
         x_copy(way).wait_send()
         corner_copy(way).wait_send()
-        for late in range(2):
+        for late in range(fringe + 1):
             y_copy(way, late).wait_send()
-
-    def drain(x, _):
-        out_copy(x).wait()
-        return 0
-
-    lax.fori_loop(0, width_x, drain, 0)
 
 
 def body(n, m, populations, precursor, pairing, rates, loading, disc_cols, disc_turb):
     comps, width_x, width_y, depth = populations.shape
     fringe = precursor.shape[1]
     rows = 10 * width_y
-    chunk = -(-rows // (n * BLOCK)) * BLOCK
+    half = n // 2
+    chunk = -(-rows // (half * BLOCK)) * BLOCK
     turbines = loading.shape[0]
     slots = disc_cols.shape[0]
     f32 = jnp.float32
-    anywhere = pl.BlockSpec(memory_space=pl.ANY)
     hbm = pl.BlockSpec(memory_space=pltpu.HBM)
     vmem = pl.BlockSpec(memory_space=pltpu.VMEM)
     dma = pltpu.SemaphoreType.DMA
     out, speed = pl.pallas_call(
         functools.partial(kernel, n, m, chunk),
         out_shape=(
-            jax.ShapeDtypeStruct(populations.shape, f32),
+            pltpu.VMEM(populations.shape, f32),
             jax.ShapeDtypeStruct((1, turbines), f32),
         ),
         in_specs=[hbm] * 7,
-        out_specs=(anywhere, vmem),
+        out_specs=(vmem, vmem),
         scratch_shapes=[
             pltpu.VMEM(populations.shape, f32),
             pltpu.VMEM(precursor.shape, f32),
@@ -442,27 +450,26 @@
             pltpu.VMEM((1, slots), jnp.int32),
             pltpu.VMEM((1, slots), jnp.int32),
             pltpu.VMEM((comps, width_x + 2, width_y, depth), f32),
-            pltpu.VMEM(populations.shape, f32),
-            pltpu.VMEM((fringe, n * chunk, depth), f32),
-            pltpu.VMEM((fringe, n, chunk, depth), f32),
-            pltpu.VMEM((fringe, n * chunk, depth), f32),
+            pltpu.VMEM((fringe, half * chunk, depth), f32),
+            pltpu.VMEM((fringe, half, chunk, depth), f32),
+            pltpu.VMEM((fringe, half * chunk, depth), f32),
             pltpu.VMEM((n, BLOCK, LANES), f32),
             pltpu.VMEM((m, BLOCK, LANES), f32),
             pltpu.VMEM((BLOCK, LANES), f32),
             pltpu.VMEM((width_x, width_y, LANES), f32),
             pltpu.VMEM((2, width_x, 16, depth), f32),
             pltpu.VMEM((2, width_x + 2, 16, depth), f32),
-            dma((fringe + 6,)), dma((width_x,)),
-            dma((fringe * n,)), dma((fringe * n,)), dma((fringe * n,)), dma((fringe * n,)),
+            dma((fringe + 6,)),
+            dma((fringe * n,)), dma((fringe * n,)), dma((fringe * half,)), dma((fringe * half,)),
             dma((n,)), dma((n,)), dma((m,)), dma((m,)),
-            dma((2,)), dma((2,)), dma((4,)), dma((4,)), dma((2,)), dma((2,)),
+            dma((2,)), dma((2,)), dma((2 * fringe + 2,)), dma((2 * fringe + 2,)), dma((2,)), dma((2,)),
         ] + [pltpu.VMEM((n, chunk, depth), f32)] * fringe,
         compiler_params=pltpu.CompilerParams(
-            collective_id=0, has_side_effects=True, vmem_limit_bytes=64 * 1024 * 1024),
-    )(
+            collective_id=0, has_side_effects=True, vmem_limit_bytes=40 * 1024 * 1024),
+    )(*(pltpu.with_memory_space_constraint(x, pltpu.HBM) for x in (
         populations, precursor, pairing, rates,
         loading.reshape(1, turbines), disc_cols.reshape(1, slots), disc_turb.reshape(1, slots),
-    )
+    )))
     return out, speed.reshape(turbines)
 
 

time: 39.8 us -> 39.7 us (level)
  local copies, waits for them, and re-layouts: 4.9 us -> 2.31 us
  Pallas kernels: 34.1 us -> 36.6 us
    unnamed x4 -> x2, local copies, waits for them, and re-layouts: 4.9 us -> 2.31 us
    pallas_call x1, Pallas kernels: 34.1 us -> 36.6 us  [body(): pl.pallas_call(functools.partial(kernel, n, m, chunk), out_shape=(pltpu.V...]
where the time goes in v3:
time: 39.7 us; the launch traced here: 39.5 us
  Pallas kernels  36.6 us (92%)
  local copies, waits for them, and re-layouts  2.31 us (6%)
  between operations  0.64 us (2%)
    pallas_call x1, Pallas kernels, body(): pl.pallas_call(functools.partial(kernel, n, m, chunk), out_shape=(pltpu.V...  36.6 us
    unnamed x2, local copies, waits for them, and re-layouts  2.31 us

profile of v3, /device:TPU:0, one launch (start us, length us, event | category | flops | bytes accessed | tf_op | source)
XLA Modules:
  0.0 39.5 jit_solution(3173166846059720345)
XLA Ops:
  0.6 36.6 %shard_map.86 = (f32[27,8,32,128]{3,2,1,0:T(8,128)S(1)}, f32[1,32]{1,0:T(1,128)S(1)}) custom-call(f32[27,8,32,128]{3,2,1,0:T(8,128)} %pops_hbm.1, f32[27,2,32,128]{3,2,1,0:T(8,128)} %prec_hbm.1, s32[8]{0:T(128)} %pairing_hbm.1, f32[27]{0:T(128)} %rates_hbm.1, f32[1,32]{1,0:T(1,128)} %bitcast.7, s32[1,512]{1,0:T(1,128)} %bitcast.5, s32[1,512]{1,0:T(1,128)} %bitcast.6), custom_call_target="tpu_custom_call" | custom-call | tf_op jit(solution)/shard_map/pallas_call | solution.py:436
  37.2 1.8 %copy.11 = f32[27,8,32,128]{3,2,1,0:T(8,128)} copy(f32[27,8,32,128]{3,2,1,0:T(8,128)S(1)} %get-tuple-element.6) | data formatting | bytes 7077888
  39.0 0.5 %copy.12 = f32[32]{0:T(128)} copy(f32[32]{0:T(128)S(1)} %bitcast.4) | data formatting | bytes 256

commit v4 on v3

--- a/solution.py
+++ b/solution.py
@@ -62,7 +62,7 @@
     return out
 
 
-def rebuild(low):
+def rebuild(low, count=27):
     rho, jx, jy, jz, xx, yy, zz, xy, xz, yz = low
     base = 2.5 * rho - 1.5 * (xx + yy + zz)
     third = rho * (1.0 / 3.0)
@@ -77,7 +77,7 @@
         return value + term if sign > 0 else value - term
 
     out = []
-    for i in range(27):
+    for i in range(count):
         steps = (i // 9 - 1, (i // 3) % 3 - 1, i % 3 - 1)
         value = base
         for d in range(3):
@@ -97,12 +97,13 @@
 def kernel(
     n, m, chunk,
     pops_hbm, prec_hbm, pairing_hbm, rates_hbm, loading_hbm, cols_hbm, turb_hbm,
-    out, speed,
+    out_any, speed,
     pops, prec, pairing, rates, loading, cols, turb,
-    post, mom, stage, final, tot_x, tot_y, load_pad, hits, ysend, yrecv,
-    in_sem, a_send, a_recv, b_send, b_recv, tx_send, tx_recv, ty_send, ty_recv,
-    x_send, x_recv, y_send, y_recv, c_send, c_recv, *got,
+    post, outv, mom, tot_x, tot_y, load_pad, hits, ysend, yrecv,
+    in_sem, out_sem, a_send, a_recv, b_send, b_recv, tx_send, tx_recv, ty_send, ty_recv,
+    x_send, x_recv, y_send, y_recv, *exchange,
 ):
+    got, stage, final = exchange[0::3], exchange[1::3], exchange[2::3]
     comps, width_x, width_y, depth = pops.shape
     fringe = prec.shape[1]
     turbines = loading.shape[1]
@@ -159,7 +160,7 @@
         other = lax.rem(place + i, half)
         slot = place if sent else other
         return pltpu.make_async_remote_copy(
-            src_ref=stage.at[p, other], dst_ref=final.at[p, span(slot), :],
+            src_ref=stage[p].at[other], dst_ref=final[p].at[:, span(slot), :],
             send_sem=b_send.at[p * half + other], recv_sem=b_recv.at[p * half + slot],
             device_id={"gx": group * half + other}, device_id_type=MESH)
 
@@ -272,12 +273,16 @@
 
         def forward_chunk(i, _):
             to = lax.rem(place + i, half)
-            stage[p, to] = got[p][pairing[group * half + to]]
+            stage[p][to, 0] = got[p][pairing[group * half + to]]
+            if p == 0:
+                stage[p][to, 1] = got[p][pairing[lax.rem(group * half + to + 1, n)]]
             second(p, i, True).start()
             return 0
 
         lax.fori_loop(1, half, forward_chunk, 0)
-        final[p, span(place), :] = got[p][pairing[me]]
+        final[p][0, span(place), :] = got[p][pairing[me]]
+        if p == 0:
+            final[p][1, span(place), :] = got[p][pairing[right]]
 
     part = -(-width_x // (fringe + 1))
     for p in range(fringe):
@@ -318,35 +323,34 @@
             src_ref=src, dst_ref=dst, send_sem=x_send.at[way], recv_sem=x_recv.at[way],
             device_id={"gx": to}, device_id_type=MESH)
 
+    def y_slot(x):
+        return lax.rem(x + 1, width_x + 2)
+
     def y_copy(way, late):
-        planes = (late - 1, 1) if late else (fringe, width_x - fringe)
+        slots = pl.ds(0, fringe + 2) if late else pl.ds(fringe + 2, width_x - fringe)
         return pltpu.make_async_remote_copy(
-            src_ref=ysend.at[way, pl.ds(planes[0], planes[1])],
-            dst_ref=yrecv.at[way, pl.ds(planes[0] + 1, planes[1])],
-            send_sem=y_send.at[(fringe + 1) * way + late], recv_sem=y_recv.at[(fringe + 1) * way + late],
+            src_ref=ysend.at[way, slots], dst_ref=yrecv.at[way, slots],
+            send_sem=y_send.at[2 * way + late], recv_sem=y_recv.at[2 * way + late],
             device_id={"gy": above if way else below}, device_id_type=MESH)
 
-    def corner_copy(way):
-        if way:
-            src, dst, to = yrecv.at[:, width_x, pl.ds(8, 8)], yrecv.at[:, 0, pl.ds(8, 8)], right
-        else:
-            src, dst, to = yrecv.at[:, 1, pl.ds(0, 8)], yrecv.at[:, width_x + 1, pl.ds(0, 8)], left
-        return pltpu.make_async_remote_copy(
-            src_ref=src, dst_ref=dst, send_sem=c_send.at[way], recv_sem=c_recv.at[way],
-            device_id={"gx": to}, device_id_type=MESH)
-
-    def pack(x, _):
+    def pack(x, kinds=(0, 1, 2)):
         for way in range(2):
             edge = width_y - 1 if way else 0
-            for kx in range(3):
+            for kx in kinds:
                 for kz in range(3):
                     row = row_of(kx, kz)
-                    ysend[way, x, row : row + 1, :] = post[
-                        9 * kx + 6 * way + kz, x + 1, edge : edge + 1, :]
+                    ysend[way, y_slot(x), row : row + 1, :] = post[
+                        9 * kx + 6 * way + kz, x, edge : edge + 1, :]
+
+    def pack_early(x, _):
+        pack(x)
         return 0
 
     lane = lax.broadcasted_iota(jnp.int32, (width_y, depth), 1)
     sub = lax.broadcasted_iota(jnp.int32, (width_y, depth), 0)
+
+    def out_copy(x):
+        return pltpu.make_async_copy(outv.at[:, x], out_any.at[:, x], out_sem.at[x])
 
     def stream(x, _):
         for i in range(27):
@@ -356,57 +360,60 @@
             if ky != 1:
                 way = 1 if ky == 2 else 0
                 row = row_of(kx, kz)
-                halo = yrecv[way, source, row : row + 1, :]
+                halo = yrecv[way, y_slot(source), row : row + 1, :]
                 moved = pltpu.roll(moved, 1 if way else width_y - 1, 0)
                 moved = jnp.where(sub == (0 if way else width_y - 1), halo, moved)
             if kz != 1:
                 moved = pltpu.roll(moved, 1 if kz == 2 else depth - 1, 1)
                 moved = jnp.where(lane == (0 if kz == 2 else depth - 1), post[26 - i, x + 1], moved)
-            out[i, x] = moved
+            outv[i, x] = moved
+        out_copy(x).start()
         return 0
 
-    x_copy(1).start()
-    lax.fori_loop(fringe, width_x, pack, 0)
+    for way in range(2):
+        x_copy(way).start()
+    lax.fori_loop(fringe + 1, width_x + 1, pack_early, 0)
     for way in range(2):
         y_copy(way, 0).start()
-
-    for p in range(fringe):
+    for way in range(2):
+        y_copy(way, 0).wait_recv()
+    lax.fori_loop(fringe + 1, width_x - 1, stream, 0)
+
+    def mix(p, table, x, count, b):
         blend = 0.5 / (p + 1.0)
+        rows = pl.ds(pl.multiple_of(b * BLOCK, BLOCK), BLOCK)
+        low = []
+        for q in range(10):
+            start = pl.multiple_of(q * width_y + b * BLOCK, BLOCK)
+            low.append(final[p][table, pl.ds(start, BLOCK), :])
+        for i, value in enumerate(rebuild(low, count)):
+            post[i, x, rows, :] = (1.0 - blend) * post[i, x, rows, :] + blend * value
+
+    def mixes(p, table, x, count):
+        def step(b, _):
+            mix(p, table, x, count, b)
+            return 0
+
+        lax.fori_loop(0, blocks, step, 0)
+
+    x_copy(1).wait_recv()
+    pack(0, (2,))
+    each(half, lambda i: second(0, i, False).wait_recv())
+    x_copy(0).wait_send()
+    mixes(0, 0, 1, 27)
+    x_copy(0).wait_recv()
+    mixes(0, 1, width_x + 1, 9)
+    pack(1)
+    pack(width_x + 1, (0,))
+    for p in range(1, fringe):
         each(half, lambda i, p=p: second(p, i, False).wait_recv())
-
-        def blend_block(b, _, p=p, blend=blend):
-            rows = pl.ds(pl.multiple_of(b * BLOCK, BLOCK), BLOCK)
-            low = []
-            for q in range(10):
-                start = pl.multiple_of(q * width_y + b * BLOCK, BLOCK)
-                low.append(final[p, pl.ds(start, BLOCK), :])
-            for i, value in enumerate(rebuild(low)):
-                post[i, p + 1, rows, :] = (1.0 - blend) * post[i, p + 1, rows, :] + blend * value
-            return 0
-
-        lax.fori_loop(0, blocks, blend_block, 0)
-        if p == 0:
-            x_copy(0).start()
-        pack(p, 0)
-        for way in range(2):
-            y_copy(way, p + 1).start()
-        if p == 0:
-            for way in range(2):
-                y_copy(way, 0).wait_recv()
-            corner_copy(1).start()
-
+        mixes(p, 0, p + 1, 27)
+        pack(p + 1)
+    for way in range(2):
+        y_copy(way, 1).start()
     for way in range(2):
         y_copy(way, 1).wait_recv()
-    corner_copy(0).start()
-    lax.fori_loop(fringe + 1, width_x - 1, stream, 0)
-    for late in range(2, fringe + 1):
-        for way in range(2):
-            y_copy(way, late).wait_recv()
-    x_copy(1).wait_recv()
-    corner_copy(1).wait_recv()
     lax.fori_loop(0, fringe + 1, stream, 0)
-    x_copy(0).wait_recv()
-    corner_copy(0).wait_recv()
     lax.fori_loop(width_x - 1, width_x, stream, 0)
 
     for p in range(fringe):
@@ -414,11 +421,16 @@
         each(half, lambda i, p=p: second(p, i, True).wait_send())
     each(n, lambda i: total_x(i, True).wait_send())
     each(m, lambda i: total_y(i, True).wait_send())
+    x_copy(1).wait_send()
     for way in range(2):
-        x_copy(way).wait_send()
-        corner_copy(way).wait_send()
-        for late in range(fringe + 1):
+        for late in range(2):
             y_copy(way, late).wait_send()
+
+    def drain(x, _):
+        out_copy(x).wait()
+        return 0
+
+    lax.fori_loop(0, width_x, drain, 0)
 
 
 def body(n, m, populations, precursor, pairing, rates, loading, disc_cols, disc_turb):
@@ -430,6 +442,7 @@
     turbines = loading.shape[0]
     slots = disc_cols.shape[0]
     f32 = jnp.float32
+    anywhere = pl.BlockSpec(memory_space=pl.ANY)
     hbm = pl.BlockSpec(memory_space=pltpu.HBM)
     vmem = pl.BlockSpec(memory_space=pltpu.VMEM)
     dma = pltpu.SemaphoreType.DMA
@@ -440,7 +453,7 @@
             jax.ShapeDtypeStruct((1, turbines), f32),
         ),
         in_specs=[hbm] * 7,
-        out_specs=(vmem, vmem),
+        out_specs=(anywhere, vmem),
         scratch_shapes=[
             pltpu.VMEM(populations.shape, f32),
             pltpu.VMEM(precursor.shape, f32),
@@ -450,20 +463,26 @@
             pltpu.VMEM((1, slots), jnp.int32),
             pltpu.VMEM((1, slots), jnp.int32),
             pltpu.VMEM((comps, width_x + 2, width_y, depth), f32),
-            pltpu.VMEM((fringe, half * chunk, depth), f32),
-            pltpu.VMEM((fringe, half, chunk, depth), f32),
+            pltpu.VMEM(populations.shape, f32),
             pltpu.VMEM((fringe, half * chunk, depth), f32),
             pltpu.VMEM((n, BLOCK, LANES), f32),
             pltpu.VMEM((m, BLOCK, LANES), f32),
             pltpu.VMEM((BLOCK, LANES), f32),
             pltpu.VMEM((width_x, width_y, LANES), f32),
-            pltpu.VMEM((2, width_x, 16, depth), f32),
             pltpu.VMEM((2, width_x + 2, 16, depth), f32),
-            dma((fringe + 6,)),
+            pltpu.VMEM((2, width_x + 2, 16, depth), f32),
+            dma((fringe + 6,)), dma((width_x,)),
             dma((fringe * n,)), dma((fringe * n,)), dma((fringe * half,)), dma((fringe * half,)),
             dma((n,)), dma((n,)), dma((m,)), dma((m,)),
-            dma((2,)), dma((2,)), dma((2 * fringe + 2,)), dma((2 * fringe + 2,)), dma((2,)), dma((2,)),
-        ] + [pltpu.VMEM((n, chunk, depth), f32)] * fringe,
+            dma((2,)), dma((2,)), dma((4,)), dma((4,)),
+        ] + [
+            pltpu.VMEM(shape, f32)
+            for p in range(fringe)
+            for shape in (
+                (n, chunk, depth),
+                (half, 1 + (p == 0), chunk, depth),
+                (1 + (p == 0), half * chunk, depth))
+        ],
         compiler_params=pltpu.CompilerParams(
             collective_id=0, has_side_effects=True, vmem_limit_bytes=40 * 1024 * 1024),
     )(*(pltpu.with_memory_space_constraint(x, pltpu.HBM) for x in (

time: 39.7 us -> 41.9 us (1.055)
  Pallas kernels: 36.6 us -> 38.4 us
    pallas_call x1, Pallas kernels: 36.6 us -> 38.4 us  [body(): pl.pallas_call(functools.partial(kernel, n, m, chunk), out_shape=(pltpu.V...]
where the time goes in v4:
time: 41.9 us; the launch traced here: 41.4 us
  Pallas kernels  38.4 us (92%)
  local copies, waits for them, and re-layouts  2.31 us (6%)
  between operations  0.64 us (2%)
    pallas_call x1, Pallas kernels, body(): pl.pallas_call(functools.partial(kernel, n, m, chunk), out_shape=(pltpu.V...  38.4 us
    unnamed x2, local copies, waits for them, and re-layouts  2.31 us

profile of v4, /device:TPU:0, one launch (start us, length us, event | category | flops | bytes accessed | tf_op | source)
XLA Modules:
  0.0 41.4 jit_solution(9662786825400612534)
XLA Ops:
  0.6 38.4 %shard_map.86 = (f32[27,8,32,128]{3,2,1,0:T(8,128)S(1)}, f32[1,32]{1,0:T(1,128)S(1)}) custom-call(f32[27,8,32,128]{3,2,1,0:T(8,128)} %pops_hbm.1, f32[27,2,32,128]{3,2,1,0:T(8,128)} %prec_hbm.1, s32[8]{0:T(128)} %pairing_hbm.1, f32[27]{0:T(128)} %rates_hbm.1, f32[1,32]{1,0:T(1,128)} %bitcast.7, s32[1,512]{1,0:T(1,128)} %bitcast.5, s32[1,512]{1,0:T(1,128)} %bitcast.6), custom_call_target="tpu_custom_call" | custom-call | tf_op jit(solution)/shard_map/pallas_call | solution.py:449
  39.0 1.8 %copy.11 = f32[27,8,32,128]{3,2,1,0:T(8,128)} copy(f32[27,8,32,128]{3,2,1,0:T(8,128)S(1)} %get-tuple-element.6) | data formatting | bytes 7077888
  40.8 0.5 %copy.12 = f32[32]{0:T(128)} copy(f32[32]{0:T(128)S(1)} %bitcast.4) | data formatting | bytes 256

commit v5 on v2

--- a/solution.py
+++ b/solution.py
@@ -428,7 +428,7 @@
     out, speed = pl.pallas_call(
         functools.partial(kernel, n, m, chunk),
         out_shape=(
-            jax.ShapeDtypeStruct(populations.shape, f32),
+            pltpu.VMEM(populations.shape, f32),
             jax.ShapeDtypeStruct((1, turbines), f32),
         ),
         in_specs=[hbm] * 7,
@@ -458,11 +458,11 @@
             dma((2,)), dma((2,)), dma((4,)), dma((4,)), dma((2,)), dma((2,)),
         ] + [pltpu.VMEM((n, chunk, depth), f32)] * fringe,
         compiler_params=pltpu.CompilerParams(
-            collective_id=0, has_side_effects=True, vmem_limit_bytes=64 * 1024 * 1024),
-    )(
+            collective_id=0, has_side_effects=True, vmem_limit_bytes=40 * 1024 * 1024),
+    )(*(pltpu.with_memory_space_constraint(x, pltpu.HBM) for x in (
         populations, precursor, pairing, rates,
         loading.reshape(1, turbines), disc_cols.reshape(1, slots), disc_turb.reshape(1, slots),
-    )
+    )))
     return out, speed.reshape(turbines)
 
 

time: 39.8 us -> 36.5 us (0.917)
  local copies, waits for them, and re-layouts: 4.9 us -> 2.31 us
  Pallas kernels: 34.1 us -> 33.4 us
    unnamed x4 -> x2, local copies, waits for them, and re-layouts: 4.9 us -> 2.31 us
    pallas_call x1, Pallas kernels: 34.1 us -> 33.4 us  [body(): pl.pallas_call(functools.partial(kernel, n, m, chunk), out_shape=(pltpu.V...]
where the time goes in v5:
time: 36.5 us; the launch traced here: 36.3 us
  Pallas kernels  33.4 us (92%)
  local copies, waits for them, and re-layouts  2.31 us (6%)
  between operations  0.64 us (2%)
    pallas_call x1, Pallas kernels, body(): pl.pallas_call(functools.partial(kernel, n, m, chunk), out_shape=(pltpu.V...  33.4 us
    unnamed x2, local copies, waits for them, and re-layouts  2.31 us

profile of v5, /device:TPU:0, one launch (start us, length us, event | category | flops | bytes accessed | tf_op | source)
XLA Modules:
  0.0 36.3 jit_solution(17866344320807712752)
XLA Ops:
  0.6 33.4 %shard_map.86 = (f32[27,8,32,128]{3,2,1,0:T(8,128)S(1)}, f32[1,32]{1,0:T(1,128)S(1)}) custom-call(f32[27,8,32,128]{3,2,1,0:T(8,128)} %pops_hbm.1, f32[27,2,32,128]{3,2,1,0:T(8,128)} %prec_hbm.1, s32[8]{0:T(128)} %pairing_hbm.1, f32[27]{0:T(128)} %rates_hbm.1, f32[1,32]{1,0:T(1,128)} %bitcast.7, s32[1,512]{1,0:T(1,128)} %bitcast.5, s32[1,512]{1,0:T(1,128)} %bitcast.6), custom_call_target="tpu_custom_call" | custom-call | tf_op jit(solution)/shard_map/pallas_call | solution.py:428
  34.0 1.8 %copy.11 = f32[27,8,32,128]{3,2,1,0:T(8,128)} copy(f32[27,8,32,128]{3,2,1,0:T(8,128)S(1)} %get-tuple-element.6) | data formatting | bytes 7077888
  35.8 0.5 %copy.12 = f32[32]{0:T(128)} copy(f32[32]{0:T(128)S(1)} %bitcast.4) | data formatting | bytes 256

commit v6 on v5

--- a/solution.py
+++ b/solution.py
@@ -228,7 +228,7 @@
         return acc + jnp.sum(velocity * profile[:1], axis=1, keepdims=True) * hits[x]
 
     acc = lax.fori_loop(0, width_x, share, jnp.zeros((width_y, LANES), jnp.float32))
-    tot_x[me] = jnp.broadcast_to(jnp.sum(acc, axis=0, keepdims=True), (BLOCK, LANES))
+    tot_x[me] = jnp.sum(acc, axis=0, keepdims=True)
     each(n, lambda i: total_x(i, True).start())
 
     def collide_block(x, b):
@@ -280,9 +280,9 @@
     norm = counts * jnp.sum(profile, axis=1, keepdims=True)
     each(m, lambda i: total_y(i, False).wait_recv())
     totals = lax.fori_loop(1, m, lambda i, t: t + tot_y[i], tot_y[0])
-    disc_speed = totals / jnp.where(counts > 0.0, norm, 1.0)
-    speed[...] = disc_speed[:1, :turbines]
-    thrust = (0.5 * load_pad[...] * disc_speed * jnp.abs(disc_speed))[:1]
+    disc_speed = totals / jnp.where(counts > 0.0, norm, 1.0)[:1]
+    speed[...] = disc_speed[:, :turbines]
+    thrust = 0.5 * load_pad[:1] * disc_speed * jnp.abs(disc_speed)
 
     def push(x, _):
         column = jnp.sum(hits[x] * thrust, axis=1, keepdims=True)
@@ -305,11 +305,11 @@
             device_id={"gx": to}, device_id_type=MESH)
 
     def y_copy(way, late):
-        planes = (0, fringe) if late else (fringe, width_x - fringe)
+        planes = (late - 1, 1) if late else (fringe, width_x - fringe)
         return pltpu.make_async_remote_copy(
             src_ref=ysend.at[way, pl.ds(planes[0], planes[1])],
             dst_ref=yrecv.at[way, pl.ds(planes[0] + 1, planes[1])],
-            send_sem=y_send.at[2 * way + late], recv_sem=y_recv.at[2 * way + late],
+            send_sem=y_send.at[(fringe + 1) * way + late], recv_sem=y_recv.at[(fringe + 1) * way + late],
             device_id={"gy": above if way else below}, device_id_type=MESH)
 
     def corner_copy(way):
@@ -377,17 +377,21 @@
         lax.fori_loop(0, blocks, blend_block, 0)
         if p == 0:
             x_copy(0).start()
-
-    lax.fori_loop(0, fringe, pack, 0)
-    for way in range(2):
-        y_copy(way, 1).start()
-    for way in range(2):
-        y_copy(way, 0).wait_recv()
-    corner_copy(1).start()
-    for way in range(2):
-        y_copy(way, 1).wait_recv()
-    corner_copy(0).start()
-    lax.fori_loop(fringe + 1, width_x - 1, stream, 0)
+        pack(p, 0)
+        for way in range(2):
+            y_copy(way, p + 1).start()
+        if p == 0:
+            for way in range(2):
+                y_copy(way, 0).wait_recv()
+            corner_copy(1).start()
+            lax.fori_loop(fringe + 1, width_x - 1, stream, 0)
+            for way in range(2):
+                y_copy(way, 1).wait_recv()
+            corner_copy(0).start()
+
+    for late in range(2, fringe + 1):
+        for way in range(2):
+            y_copy(way, late).wait_recv()
     x_copy(1).wait_recv()
     corner_copy(1).wait_recv()
     lax.fori_loop(0, fringe + 1, stream, 0)
@@ -403,7 +407,7 @@
     for way in range(2):
         x_copy(way).wait_send()
         corner_copy(way).wait_send()
-        for late in range(2):
+        for late in range(fringe + 1):
             y_copy(way, late).wait_send()
 
     def drain(x, _):
@@ -446,8 +450,8 @@
             pltpu.VMEM((fringe, n * chunk, depth), f32),
             pltpu.VMEM((fringe, n, chunk, depth), f32),
             pltpu.VMEM((fringe, n * chunk, depth), f32),
-            pltpu.VMEM((n, BLOCK, LANES), f32),
-            pltpu.VMEM((m, BLOCK, LANES), f32),
+            pltpu.VMEM((n, 1, LANES), f32),
+            pltpu.VMEM((m, 1, LANES), f32),
             pltpu.VMEM((BLOCK, LANES), f32),
             pltpu.VMEM((width_x, width_y, LANES), f32),
             pltpu.VMEM((2, width_x, 16, depth), f32),
@@ -455,7 +459,7 @@
             dma((fringe + 6,)), dma((width_x,)),
             dma((fringe * n,)), dma((fringe * n,)), dma((fringe * n,)), dma((fringe * n,)),
             dma((n,)), dma((n,)), dma((m,)), dma((m,)),
-            dma((2,)), dma((2,)), dma((4,)), dma((4,)), dma((2,)), dma((2,)),
+            dma((2,)), dma((2,)), dma((2 * fringe + 2,)), dma((2 * fringe + 2,)), dma((2,)), dma((2,)),
         ] + [pltpu.VMEM((n, chunk, depth), f32)] * fringe,
         compiler_params=pltpu.CompilerParams(
             collective_id=0, has_side_effects=True, vmem_limit_bytes=40 * 1024 * 1024),

time: 36.5 us -> 35.1 us (0.962)
  Pallas kernels: 33.4 us -> 32 us
    pallas_call x1, Pallas kernels: 33.4 us -> 32 us  [body(): pl.pallas_call(functools.partial(kernel, n, m, chunk), out_shape=(pltpu.V...]
where the time goes in v6:
time: 35.1 us; the launch traced here: 34.9 us
  Pallas kernels  32 us (91%)
  local copies, waits for them, and re-layouts  2.31 us (7%)
  between operations  0.64 us (2%)
    pallas_call x1, Pallas kernels, body(): pl.pallas_call(functools.partial(kernel, n, m, chunk), out_shape=(pltpu.V...  32 us
    unnamed x2, local copies, waits for them, and re-layouts  2.31 us

profile of v6, /device:TPU:0, one launch (start us, length us, event | category | flops | bytes accessed | tf_op | source)
XLA Modules:
  0.0 34.9 jit_solution(18372876109037188526)
XLA Ops:
  0.6 32.0 %shard_map.86 = (f32[27,8,32,128]{3,2,1,0:T(8,128)S(1)}, f32[1,32]{1,0:T(1,128)S(1)}) custom-call(f32[27,8,32,128]{3,2,1,0:T(8,128)} %pops_hbm.1, f32[27,2,32,128]{3,2,1,0:T(8,128)} %prec_hbm.1, s32[8]{0:T(128)} %pairing_hbm.1, f32[27]{0:T(128)} %rates_hbm.1, f32[1,32]{1,0:T(1,128)} %bitcast.7, s32[1,512]{1,0:T(1,128)} %bitcast.5, s32[1,512]{1,0:T(1,128)} %bitcast.6), custom_call_target="tpu_custom_call" | custom-call | tf_op jit(solution)/shard_map/pallas_call | solution.py:432
  32.6 1.8 %copy.11 = f32[27,8,32,128]{3,2,1,0:T(8,128)} copy(f32[27,8,32,128]{3,2,1,0:T(8,128)S(1)} %get-tuple-element.6) | data formatting | bytes 7077888
  34.4 0.5 %copy.12 = f32[32]{0:T(128)} copy(f32[32]{0:T(128)S(1)} %bitcast.4) | data formatting | bytes 256

commit v7 on v6

--- a/solution.py
+++ b/solution.py
@@ -417,6 +417,33 @@
     lax.fori_loop(0, width_x, drain, 0)
 
 
+def deliver_kernel(out_from, speed_from, out_to, speed_to, sems):
+    count = out_from.shape[0]
+
+    def copy(i):
+        return pltpu.make_async_copy(out_from.at[i], out_to.at[i], sems.at[i])
+
+    copies = [copy(i) for i in range(count)]
+    copies.append(pltpu.make_async_copy(speed_from, speed_to, sems.at[count]))
+    for item in copies:
+        item.start()
+    for item in copies:
+        item.wait()
+
+
+def deliver(out, speed, turbines):
+    anywhere = pl.BlockSpec(memory_space=pl.ANY)
+    vmem = pltpu.VMEM
+    out, speed = pl.pallas_call(
+        deliver_kernel,
+        out_shape=(pltpu.HBM(out.shape, out.dtype), pltpu.HBM(speed.shape, speed.dtype)),
+        in_specs=[anywhere, anywhere],
+        out_specs=(anywhere, anywhere),
+        scratch_shapes=[pltpu.SemaphoreType.DMA((out.shape[0] + 1,))],
+    )(pltpu.with_memory_space_constraint(out, vmem), pltpu.with_memory_space_constraint(speed, vmem))
+    return out, speed.reshape(turbines)
+
+
 def body(n, m, populations, precursor, pairing, rates, loading, disc_cols, disc_turb):
     comps, width_x, width_y, depth = populations.shape
     fringe = precursor.shape[1]
@@ -433,7 +460,7 @@
         functools.partial(kernel, n, m, chunk),
         out_shape=(
             pltpu.VMEM(populations.shape, f32),
-            jax.ShapeDtypeStruct((1, turbines), f32),
+            pltpu.VMEM((1, turbines), f32),
         ),
         in_specs=[hbm] * 7,
         out_specs=(anywhere, vmem),
@@ -467,7 +494,7 @@
         populations, precursor, pairing, rates,
         loading.reshape(1, turbines), disc_cols.reshape(1, slots), disc_turb.reshape(1, slots),
     )))
-    return out, speed.reshape(turbines)
+    return deliver(out, speed, turbines)
 
 
 def solution(mesh):

time: 35.1 us -> 34.8 us (level)
  local copies, waits for them, and re-layouts: 2.31 us -> 0 us
  Pallas kernels: 32 us -> 34 us
    unnamed x2 -> x0, local copies, waits for them, and re-layouts: 2.31 us -> none
    pallas_call x0 -> x1, Pallas kernels: none -> 2.02 us  [deliver(): pl.pallas_call(deliver_kernel, out_shape=(pltpu.HBM(out.shape, out.dtype)...]
where the time goes in v7:
time: 34.8 us; the launch traced here: 34.6 us
  Pallas kernels  34 us (98%)
  between operations  0.64 us (2%)
    pallas_call x1, Pallas kernels, body(): pl.pallas_call(functools.partial(kernel, n, m, chunk), out_shape=(pltpu.V...  32 us
    pallas_call x1, Pallas kernels, deliver(): pl.pallas_call(deliver_kernel, out_shape=(pltpu.HBM(out.shape, out.dtype)...  2.02 us

profile of v7, /device:TPU:0, one launch (start us, length us, event | category | flops | bytes accessed | tf_op | source)
XLA Modules:
  0.0 34.6 jit_solution(13359065825487145792)
XLA Ops:
  0.6 32.0 %shard_map.86 = (f32[27,8,32,128]{3,2,1,0:T(8,128)S(1)}, f32[1,32]{1,0:T(1,128)S(1)}) custom-call(f32[27,8,32,128]{3,2,1,0:T(8,128)} %pops_hbm.1, f32[27,2,32,128]{3,2,1,0:T(8,128)} %prec_hbm.1, s32[8]{0:T(128)} %pairing_hbm.1, f32[27]{0:T(128)} %rates_hbm.1, f32[1,32]{1,0:T(1,128)} %bitcast.6, s32[1,512]{1,0:T(1,128)} %bitcast.4, s32[1,512]{1,0:T(1,128)} %bitcast.5), custom_call_target="tpu_custom_call" | custom-call | tf_op jit(solution)/shard_map/pallas_call | solution.py:459
  32.6 2.0 %shard_map.87 = (f32[27,8,32,128]{3,2,1,0:T(8,128)}, f32[1,32]{1,0:T(1,128)}) custom-call(f32[27,8,32,128]{3,2,1,0:T(8,128)S(1)} %get-tuple-element.6.out_from, f32[1,32]{1,0:T(1,128)S(1)} %get-tuple-element.7.speed_from), custom_call_target="tpu_custom_call" | custom-call | tf_op jit(solution)/shard_map/pallas_call | solution.py:437

commit v8 on v7

--- a/solution.py
+++ b/solution.py
@@ -119,7 +119,7 @@
             (cols_hbm, cols), (turb_hbm, turb), (pairing_hbm, pairing), (rates_hbm, rates),
             (loading_hbm, loading)))]
     pops_in = pltpu.make_async_copy(pops_hbm, pops, in_sem.at[fringe])
-    for copy in prec_in + small_in + [pops_in]:
+    for copy in prec_in + small_in:
         copy.start()
 
     barrier = pltpu.get_barrier_semaphore()
@@ -141,8 +141,11 @@
     def span(j):
         return pl.ds(pl.multiple_of(j * chunk, BLOCK), chunk)
 
+    def partner(i):
+        return lax.rem(me + n // 2 + (i // 2) * (1 - 2 * lax.rem(i, 2)) + n, n)
+
     def first(p, i, sent):
-        other = lax.rem(me + i, n)
+        other = partner(i)
         slot = me if sent else other
         return pltpu.make_async_remote_copy(
             src_ref=mom.at[p, span(other), :], dst_ref=got[p].at[slot],
@@ -150,7 +153,7 @@
             device_id={"gx": other}, device_id_type=MESH)
 
     def second(p, i, sent):
-        other = lax.rem(me + i, n)
+        other = partner(i)
         slot = me if sent else other
         return pltpu.make_async_remote_copy(
             src_ref=stage.at[p, other], dst_ref=final.at[p, span(slot), :],
@@ -180,9 +183,10 @@
 
         lax.fori_loop(1, count, step, 0)
 
+    for copy in prec_in:
+        copy.wait()
+    pops_in.start()
     for p in range(fringe):
-        prec_in[p].wait()
-
         def precursor_block(b, _, p=p):
             rows = pl.ds(pl.multiple_of(b * BLOCK, BLOCK), BLOCK)
             moments = forward([prec[i, p, rows, :] for i in range(27)])
@@ -257,7 +261,7 @@
         each(n, lambda i: first(p, i, False).wait_recv())
 
         def forward_chunk(i, _):
-            to = lax.rem(me + i, n)
+            to = partner(i)
             stage[p, to] = got[p][pairing[to]]
             second(p, i, True).start()
             return 0

time: 34.8 us -> 34.9 us (level)
  no operation moved by 1% of the time
where the time goes in v8:
time: 34.9 us; the launch traced here: 34.8 us
  Pallas kernels  34.1 us (98%)
  between operations  0.64 us (2%)
    pallas_call x1, Pallas kernels, body(): pl.pallas_call(functools.partial(kernel, n, m, chunk), out_shape=(pltpu.V...  32.1 us
    pallas_call x1, Pallas kernels, deliver(): pl.pallas_call(deliver_kernel, out_shape=(pltpu.HBM(out.shape, out.dtype)...  2.02 us

profile of v8, /device:TPU:0, one launch (start us, length us, event | category | flops | bytes accessed | tf_op | source)
XLA Modules:
  0.0 34.8 jit_solution(728619940055273287)
XLA Ops:
  0.6 32.1 %shard_map.86 = (f32[27,8,32,128]{3,2,1,0:T(8,128)S(1)}, f32[1,32]{1,0:T(1,128)S(1)}) custom-call(f32[27,8,32,128]{3,2,1,0:T(8,128)} %pops_hbm.1, f32[27,2,32,128]{3,2,1,0:T(8,128)} %prec_hbm.1, s32[8]{0:T(128)} %pairing_hbm.1, f32[27]{0:T(128)} %rates_hbm.1, f32[1,32]{1,0:T(1,128)} %bitcast.6, s32[1,512]{1,0:T(1,128)} %bitcast.4, s32[1,512]{1,0:T(1,128)} %bitcast.5), custom_call_target="tpu_custom_call" | custom-call | tf_op jit(solution)/shard_map/pallas_call | solution.py:463
  32.8 2.0 %shard_map.87 = (f32[27,8,32,128]{3,2,1,0:T(8,128)}, f32[1,32]{1,0:T(1,128)}) custom-call(f32[27,8,32,128]{3,2,1,0:T(8,128)S(1)} %get-tuple-element.6.out_from, f32[1,32]{1,0:T(1,128)S(1)} %get-tuple-element.7.speed_from), custom_call_target="tpu_custom_call" | custom-call | tf_op jit(solution)/shard_map/pallas_call | solution.py:441

commit v9 on v7

--- a/solution.py
+++ b/solution.py
@@ -267,13 +267,14 @@
 
     part = -(-width_x // (fringe + 1))
     for p in range(fringe):
-        collide(p * part, (p + 1) * part)
+        if p:
+            collide((p - 1) * part, p * part)
         pass_on(p)
 
     each(n, lambda i: total_x(i, False).wait_recv())
     tot_y[my] = lax.fori_loop(1, n, lambda i, t: t + tot_x[i], tot_x[0])
     each(m, lambda i: total_y(i, True).start())
-    collide(fringe * part, width_x)
+    collide((fringe - 1) * part, width_x)
 
     load_pad[...] = jnp.zeros((BLOCK, LANES), jnp.float32)
     load_pad[:, :turbines] = jnp.broadcast_to(loading[...], (BLOCK, turbines))

time: 34.8 us -> 34.8 us (level)
  no operation moved by 1% of the time
where the time goes in v9:
time: 34.8 us; the launch traced here: 34.6 us
  Pallas kernels  34 us (98%)
  between operations  0.64 us (2%)
    pallas_call x1, Pallas kernels, body(): pl.pallas_call(functools.partial(kernel, n, m, chunk), out_shape=(pltpu.V...  32 us
    pallas_call x1, Pallas kernels, deliver(): pl.pallas_call(deliver_kernel, out_shape=(pltpu.HBM(out.shape, out.dtype)...  2.02 us

profile of v9, /device:TPU:0, one launch (start us, length us, event | category | flops | bytes accessed | tf_op | source)
XLA Modules:
  0.0 34.6 jit_solution(7504786223850383680)
XLA Ops:
  0.6 32.0 %shard_map.86 = (f32[27,8,32,128]{3,2,1,0:T(8,128)S(1)}, f32[1,32]{1,0:T(1,128)S(1)}) custom-call(f32[27,8,32,128]{3,2,1,0:T(8,128)} %pops_hbm.1, f32[27,2,32,128]{3,2,1,0:T(8,128)} %prec_hbm.1, s32[8]{0:T(128)} %pairing_hbm.1, f32[27]{0:T(128)} %rates_hbm.1, f32[1,32]{1,0:T(1,128)} %bitcast.6, s32[1,512]{1,0:T(1,128)} %bitcast.4, s32[1,512]{1,0:T(1,128)} %bitcast.5), custom_call_target="tpu_custom_call" | custom-call | tf_op jit(solution)/shard_map/pallas_call | solution.py:460
  32.6 2.0 %shard_map.87 = (f32[27,8,32,128]{3,2,1,0:T(8,128)}, f32[1,32]{1,0:T(1,128)}) custom-call(f32[27,8,32,128]{3,2,1,0:T(8,128)S(1)} %get-tuple-element.6.out_from, f32[1,32]{1,0:T(1,128)S(1)} %get-tuple-element.7.speed_from), custom_call_target="tpu_custom_call" | custom-call | tf_op jit(solution)/shard_map/pallas_call | solution.py:438
